TPU v7x, 256 devices: a whole 4x4x8 slice. The times are simulated.
256 devices in a mesh: ctx: 16 (over x_hi, z), resp: 16 (over y, x_lo, core).
Axes of the slice: x: 4 (x_hi: 2, x_lo: 2; x = x_hi * 2 + x_lo), y: 4, z: 8, core: 2. Of those that a mesh axis runs over, the one named last changes fastest.
Arguments:
- q_resp: bfloat16 [16, 2048, 2048], P('resp', 'ctx'), may hold values from -8 to 8
- k_resp: bfloat16 [16, 2048, 512], P('resp', 'ctx'), may hold values from -6 to 6
- v_resp: bfloat16 [16, 2048, 512], P('resp', 'ctx'), may hold values from -6 to 6
- k_prompt: bfloat16 [1024, 512], P('ctx'), may hold values from -8 to 8
- v_prompt: bfloat16 [1024, 512], P('ctx'), may hold values from -6 to 6
- d_out: bfloat16 [16, 2048, 2048], P('resp', 'ctx'), may hold values from -4 to 4
- lengths: int32 [16], P('resp'), may hold values from 512 to 2048, as said below
- counts: int32 [16], P('resp'), may hold values from 256 to 2048, as said below
Outputs:
- attn_out: bfloat16 [16, 2048, 2048], P('resp', 'ctx')
- d_query: bfloat16 [16, 2048, 2048], P('resp', 'ctx')
- d_key_resp: bfloat16 [16, 2048, 512], P('resp', 'ctx')
- d_value_resp: bfloat16 [16, 2048, 512], P('resp', 'ctx')
- d_key_prompt: bfloat16 [1024, 512], P('ctx')
- d_value_prompt: bfloat16 [1024, 512], P('ctx')
Inputs may be any that keep to these rules, and one draw needn't show every extreme that they name: Rows of response r from lengths[r] on are padding; some response has 2048 real tokens. The first counts[r] tokens of response r enter the loss; (lengths[r] + 1) // 2 <= counts[r] <= lengths[r].
All inputs are finite; a program needn't handle non-finite values.
Results may differ from a plain program's by a relative error of at most 0.035.
Values may be sent and summed in bfloat16 or wider, within the bound.
No kernel may reach another device: no remote copies, remote signals or barrier semaphores. Data moves between devices by JAX's collectives and lax.ppermute only.
A program may use at most 128 MiB of HBM per device.

v0:
```python
import jax
import jax.numpy as jnp
from jax import lax
from jax.sharding import PartitionSpec as P

HEADS = 16
KV_HEADS = 4
HEAD_DIM = 128


NEG = -1e30


def block_of(source, step_index, block_size):
    return lax.dynamic_slice_in_dim(source, step_index * block_size, block_size, 0)


def attend(
    queries,
    grads_in,
    row_start,
    length,
    loss_count,
    resp_total,
    prompt_k,
    prompt_v,
    own_k,
    own_v,
    prompt_buf,
    resp_buf,
):
    row_count = queries.shape[0]
    key_heads = KV_HEADS
    group_size = HEADS // KV_HEADS
    head_width = HEAD_DIM
    score_scale = HEAD_DIM ** (-0.5)
    query_heads = queries.reshape(row_count, key_heads, group_size, head_width)
    position = row_start + jnp.arange(row_count, dtype=jnp.int32)
    prompt_block = min(512, prompt_k.shape[0])
    resp_block = min(512, resp_total)
    prompt_steps = prompt_k.shape[0] // prompt_block
    resp_steps = (row_start + row_count - 1) // resp_block + 1

    def scores(key_block, key_start, causal):
        key_split = key_block.reshape(key_block.shape[0], key_heads, head_width)
        logits = (
            jnp.einsum("ngtd,kgd->ngtk", query_heads, key_split, preferred_element_type=jnp.float32)
            * score_scale
        )
        if causal:
            key_position = key_start + jnp.arange(key_block.shape[0], dtype=jnp.int32)
            allowed = key_position[None, :] <= position[:, None]
            logits = jnp.where(allowed[:, None, None, :], logits, NEG)
        return logits

    def forward_step(flash_state, key_block, value_block, key_start, causal):
        running, totals, accumulated = flash_state
        logits = scores(key_block, key_start, causal)
        newmax = jnp.maximum(running, jnp.max(logits, axis=-1))
        factor = jnp.exp(running - newmax)
        weights = jnp.exp(logits - newmax[..., None])
        totals = totals * factor + jnp.sum(weights, axis=-1)
        value_split = value_block.reshape(value_block.shape[0], key_heads, head_width)
        accumulated = accumulated * factor[..., None] + jnp.einsum(
            "ngtk,kgd->ngtd",
            weights.astype(jnp.bfloat16),
            value_split,
            preferred_element_type=jnp.float32,
        )
        return (newmax, totals, accumulated)

    def prompt_forward(step_index, flash_state):
        return forward_step(
            flash_state,
            block_of(prompt_k, step_index, prompt_block),
            block_of(prompt_v, step_index, prompt_block),
            0,
            False,
        )

    def resp_forward(step_index, flash_state):
        return forward_step(
            flash_state,
            block_of(own_k, step_index, resp_block),
            block_of(own_v, step_index, resp_block),
            step_index * resp_block,
            True,
        )

    flash_state = (
        jnp.full((row_count, key_heads, group_size), NEG, jnp.float32),
        jnp.zeros((row_count, key_heads, group_size), jnp.float32),
        jnp.zeros((row_count, key_heads, group_size, head_width), jnp.float32),
    )
    flash_state = lax.fori_loop(0, prompt_steps, prompt_forward, flash_state)
    flash_state = lax.fori_loop(0, resp_steps, resp_forward, flash_state)
    running, totals, accumulated = flash_state
    valid_rows = (position < length).astype(jnp.float32)
    attended = (accumulated / totals[..., None] * valid_rows[:, None, None, None]).astype(
        jnp.bfloat16
    )
    log_total = running + jnp.log(totals)
    weight = jnp.where(position < loss_count, resp_total / loss_count.astype(jnp.float32), 0.0)
    upstream = (grads_in.astype(jnp.float32) * weight[:, None]).astype(jnp.bfloat16)
    up_heads = upstream.reshape(row_count, key_heads, group_size, head_width)
    row_delta = jnp.sum(up_heads.astype(jnp.float32) * attended.astype(jnp.float32), axis=-1)

    def backward_step(carried, key_block, value_block, key_start, causal):
        query_grad, buffer = carried
        block_size = key_block.shape[0]
        logits = scores(key_block, key_start, causal)
        probability = jnp.exp(logits - log_total[..., None])
        key_split = key_block.reshape(block_size, key_heads, head_width)
        value_split = value_block.reshape(block_size, key_heads, head_width)
        value_grad = jnp.einsum(
            "ngtk,ngtd->kgd",
            probability.astype(jnp.bfloat16),
            up_heads,
            preferred_element_type=jnp.float32,
        )
        prob_grad = jnp.einsum(
            "ngtd,kgd->ngtk", up_heads, value_split, preferred_element_type=jnp.float32
        )
        score_grad = (probability * (prob_grad - row_delta[..., None]) * score_scale).astype(
            jnp.bfloat16
        )
        query_grad = query_grad + jnp.einsum(
            "ngtk,kgd->ngtd", score_grad, key_split, preferred_element_type=jnp.float32
        )
        key_grad = jnp.einsum(
            "ngtk,ngtd->kgd", score_grad, query_heads, preferred_element_type=jnp.float32
        )
        update = jnp.concatenate(
            [
                key_grad.reshape(block_size, key_heads * head_width),
                value_grad.reshape(block_size, key_heads * head_width),
            ],
            axis=1,
        )
        current = lax.dynamic_slice_in_dim(buffer, key_start, block_size, 0)
        buffer = lax.dynamic_update_slice_in_dim(buffer, current + update, key_start, 0)
        return (query_grad, buffer)

    def prompt_backward(step_index, carried):
        query_grad, buffer, other = carried
        query_grad, buffer = backward_step(
            (query_grad, buffer),
            block_of(prompt_k, step_index, prompt_block),
            block_of(prompt_v, step_index, prompt_block),
            step_index * prompt_block,
            False,
        )
        return (query_grad, buffer, other)

    def resp_backward(step_index, carried):
        query_grad, other, buffer = carried
        query_grad, buffer = backward_step(
            (query_grad, buffer),
            block_of(own_k, step_index, resp_block),
            block_of(own_v, step_index, resp_block),
            step_index * resp_block,
            True,
        )
        return (query_grad, other, buffer)

    carried = (
        jnp.zeros((row_count, key_heads, group_size, head_width), jnp.float32),
        prompt_buf,
        resp_buf,
    )
    carried = lax.fori_loop(0, prompt_steps, prompt_backward, carried)
    carried = lax.fori_loop(0, resp_steps, resp_backward, carried)
    query_grad, prompt_buf, resp_buf = carried
    width_q = key_heads * group_size * head_width
    return (
        attended.reshape(row_count, width_q),
        query_grad.astype(jnp.bfloat16).reshape(row_count, width_q),
        prompt_buf,
        resp_buf,
    )


def body(q_resp, k_resp, v_resp, k_prompt, v_prompt, d_out, lengths, counts):
    ctx_count = lax.axis_size("ctx")
    ctx_index = lax.axis_index("ctx")
    row_count = q_resp.shape[1]
    resp_total = row_count * ctx_count
    width_kv = k_resp.shape[2]
    prompt_k, prompt_v = (
        lax.all_gather(k_prompt, "ctx", axis=0, tiled=True),
        lax.all_gather(v_prompt, "ctx", axis=0, tiled=True),
    )
    own_k, own_v = (
        lax.all_gather(k_resp[0], "ctx", axis=0, tiled=True),
        lax.all_gather(v_resp[0], "ctx", axis=0, tiled=True),
    )
    length = lengths[0]
    loss_count = counts[0]
    queries = q_resp[0]
    grads_in = d_out[0]
    prompt_buf = jnp.zeros((prompt_k.shape[0], 2 * width_kv), jnp.float32)
    resp_buf = jnp.zeros((resp_total, 2 * width_kv), jnp.float32)
    attended, query_grad, prompt_buf, resp_buf = attend(
        queries,
        grads_in,
        ctx_index * row_count,
        length,
        loss_count,
        resp_total,
        prompt_k,
        prompt_v,
        own_k,
        own_v,
        prompt_buf,
        resp_buf,
    )
    prompt_share, resp_final = (
        lax.psum_scatter(prompt_buf, "ctx", scatter_dimension=0, tiled=True),
        lax.psum_scatter(resp_buf, "ctx", scatter_dimension=0, tiled=True),
    )
    prompt_final = lax.psum(prompt_share, "resp").astype(jnp.bfloat16)
    resp_final = resp_final.astype(jnp.bfloat16)
    return (
        attended[None],
        query_grad[None],
        resp_final[:, :width_kv][None],
        resp_final[:, width_kv:][None],
        prompt_final[:, :width_kv],
        prompt_final[:, width_kv:],
    )


def solution(mesh):
    return jax.shard_map(
        body,
        mesh=mesh,
        in_specs=(
            P("resp", "ctx", None),
            P("resp", "ctx", None),
            P("resp", "ctx", None),
            P("ctx", None),
            P("ctx", None),
            P("resp", "ctx", None),
            P("resp"),
            P("resp"),
        ),
        out_specs=(
            P("resp", "ctx", None),
            P("resp", "ctx", None),
            P("resp", "ctx", None),
            P("resp", "ctx", None),
            P("ctx", None),
            P("ctx", None),
        ),
        check_vma=False,
    )
```

profile of v0, /device:TPU:1, one launch (start us, length us, event | category | flops | bytes accessed | tf_op | source)
XLA Modules:
  0.0 833.8 jit_solution(8938375855229511888)
XLA Ops:
  8.7 1.7 copy.90
  10.4 1.7 copy.91
  16.5 73.0 %all-gather.7.cloned.1.call-done = bf16[1024,512]{1,0:T(8,128)(2,1)} async-done(((bf16[64,512]{1,0:T(8,128)(2,1)}), bf16[1024,512]{1,0:T(8,128)(2,1)}) %all-gather.7.cloned.1.call-update) | async-done | bytes 1048592 | tf_op jit(solution)/shard_map/all_gather | solution.py:190
  89.5 2.3 copy.87
  91.8 75.7 %all-gather.9.cloned.1.call-done = bf16[1024,512]{1,0:T(8,128)(2,1)} async-done(((bf16[64,512]{1,0:T(8,128)(2,1)}), bf16[1024,512]{1,0:T(8,128)(2,1)}) %all-gather.9.cloned.1.call-update) | async-done | bytes 1048592 | tf_op jit(solution)/shard_map/all_gather | solution.py:191
  167.5 2.3 copy.89
  169.7 8.0 while.64
  177.7 75.1 %all-gather.11.cloned.1.call-done = bf16[1,2048,512]{1,2,0:T(8,128)(2,1)} async-done(((bf16[1,128,512]{1,2,0:T(8,128)(2,1)}), bf16[1,2048,512]{1,2,0:T(8,128)(2,1)}) %all-gather.11.cloned.1.call-update) | async-done | bytes 2097168 | tf_op jit(solution)/shard_map/all_gather | solution.py:194
  252.8 84.5 %all-gather.13.cloned.1.call-done = bf16[1,2048,512]{1,2,0:T(8,128)(2,1)} async-done(((bf16[1,128,512]{1,2,0:T(8,128)(2,1)}), bf16[1,2048,512]{1,2,0:T(8,128)(2,1)}) %all-gather.13.cloned.1.call-update) | async-done | bytes 2097168 | tf_op jit(solution)/shard_map/all_gather | solution.py:195
  337.3 4.8 while.62
  343.4 2.5 broadcast_in_dim.73.clone
  345.9 35.2 %while.65 = (s32[]{:T(128)}, f32[128,4,4,128]{0,3,2,1:T(8,128)}, f32[1024,1024]{1,0:T(8,128)}, bf16[1024,512]{0,1:T(8,128)(2,1)}, bf16[128,4,4,128]{0,3,2,1:T(8,...) while((s32[]{:T(128)}, f32[128,4,4,128]{0,3,2,1:T(8,128)}, ...), condition=%wide.region_10.11_spmd.clone, body=%wide.region_9.10_spmd.clone.sunk | while | flops 1353187328 | bytes 64512312 | solution.py:171
  345.9 2.1 constant_dynamic-slice_fusion.20
  348.0 3.2 constant_dynamic-slice_fusion.21
  351.1 1.9 copy.153
  358.2 1.8 maximum_add_fusion.5
  360.0 1.9 copy.154
  363.5 2.1 constant_dynamic-slice_fusion.20
  365.6 3.2 constant_dynamic-slice_fusion.21
  368.7 1.9 copy.153
  375.8 1.8 maximum_add_fusion.5
  377.6 1.9 copy.154
  381.1 4.3 broadcast_in_dim.76.clone
  385.4 18.1 %while.63 = (s32[]{:T(128)}, f32[128,4,4,128]{0,3,2,1:T(8,128)}, f32[2048,1024]{1,0:T(8,128)}, s32[]{:T(128)}, bf16[2048,512]{0,1:T(8,128)(2,1)}, /*index=5*/bf1...) while((s32[]{:T(128)}, f32[128,4,4,128]{0,3,2,1:T(8,128)}, ...), condition=%wide.region_12.13_spmd.clone, body=%wide.region_11.12_spmd.clone.sunk | while | flops 1355088512 | bytes 64714044 | solution.py:172
  385.6 2.1 constant_dynamic-slice_fusion.17
  387.7 3.2 constant_dynamic-slice_fusion.18
  390.8 1.9 copy.151
  398.3 1.8 maximum_add_fusion.4
  400.1 1.9 copy.152
  406.6 191.9 %reduce-scatter.5.cloned.1.call-done = f32[64,1024]{1,0:T(8,128)} async-done(((f32[1024,1024]{1,0:T(8,128)}), f32[64,1024]{1,0:T(8,128)}) %reduce-scatter.5.cloned.1.call-update) | async-done | bytes 262160 | tf_op jit(solution)/shard_map/reduce_scatter | solution.py:218
  598.5 57.4 %all-reduce.1 = bf16[64,1024]{1,0:T(8,128)(2,1)S(1)} all-reduce(f32[64,1024]{1,0:T(8,128)} %reduce-scatter.5.cloned.1.call-done), channel_id=1, replica_groups=mesh['ctx'=16,'resp'=16] {'resp'}, use_global_device_ids=true, to_apply=%region_15.16 | all-reduce | flops 65536 | bytes 393216 | tf_op jit(solution)/shard_map/psum | solution.py:221
  656.6 168.6 %reduce-scatter.3.cloned.1.call-done = f32[128,1024]{1,0:T(8,128)} async-done(((f32[2048,1024]{1,0:T(8,128)}), f32[128,1024]{1,0:T(8,128)}) %reduce-scatter.3.cloned.1.call-update) | async-done | bytes 524304 | tf_op jit(solution)/shard_map/reduce_scatter | solution.py:219
  (102 shorter events, 44.0 us)
Async XLA Ops:
  7.2 82.3 %all-gather.7.cloned.1.call-start = ((), (), s32[]{:S(2)}) async-start(), calls=%async_computation.2 | async-start | bytes 1114112 | tf_op jit(solution)/shard_map/all_gather | solution.py:190
  7.9 159.6 %all-gather.9.cloned.1.call-start = ((), (), s32[]{:S(2)}) async-start(), calls=%async_computation.3 | async-start | bytes 1114112 | tf_op jit(solution)/shard_map/all_gather | solution.py:191
  8.7 244.1 %all-gather.11.cloned.1.call-start = ((), (), s32[]{:S(2)}) async-start(), calls=%async_computation.6 | async-start | bytes 2228224 | tf_op jit(solution)/shard_map/all_gather | solution.py:194
  10.4 326.9 %all-gather.13.cloned.1.call-start = ((), (), s32[]{:S(2)}) async-start(), calls=%async_computation.7 | async-start | bytes 2228224 | tf_op jit(solution)/shard_map/all_gather | solution.py:195
  12.1 586.4 %reduce-scatter.5.cloned.1.call-start = ((), (), s32[]{:S(2)}) async-start(), calls=%async_computation.5 | async-start | bytes 4456448 | tf_op jit(solution)/shard_map/reduce_scatter | solution.py:218
  353.1 1.0 copy-start.5
  354.1 1.0 copy-start.7
  355.2 1.5 copy-start
  357.2 1.0 copy-start.1
  370.7 1.0 copy-start.5
  371.7 1.0 copy-start.7
  372.8 1.5 copy-start
  374.9 1.0 copy-start.1
  381.1 444.1 %reduce-scatter.3.cloned.1.call-start = ((), (), s32[]{:S(2)}) async-start(), calls=%async_computation.4 | async-start | bytes 8912896 | tf_op jit(solution)/shard_map/reduce_scatter | solution.py:219
  392.8 1.0 copy-start.6
  393.8 1.2 copy-start.8
  395.0 1.6 copy-start.2
  397.3 1.0 copy-start.3
  403.5 1.0 copy-start.9
  403.5 2.0 copy-start.4
Sparse Core Ops, SparseCore 0:
  10.6 78.8 all-gather.6
  92.1 75.3 all-gather.8
  170.5 82.1 all-gather.10
  255.7 81.6 all-gather.12
  381.2 217.2 reduce-scatter.4
  603.1 222.0 reduce-scatter.2
where the time goes:
time: 839 us; the launch traced here: 834 us
  waiting for transfers between devices  670 us (80%)
  local copies, waits for them, and re-layouts  59.1 us (7%)
  blocking collectives  57.4 us (7%)
  matrix products  20.1 us (2%)
  between operations  15.6 us (2%)
  other arithmetic  10.6 us (1%)
    reduce_scatter x1, waiting for transfers between devices, body(): lax.psum_scatter(prompt_buf, 'ctx', scatter_dimension=0, tiled=True)  192 us
    reduce_scatter x1, waiting for transfers between devices, body(): lax.psum_scatter(resp_buf, 'ctx', scatter_dimension=0, tiled=True)  169 us
    all_gather x1, waiting for transfers between devices, body(): lax.all_gather(v_resp[0], 'ctx', axis=0, tiled=True)  84.5 us
    all_gather x1, waiting for transfers between devices, body(): lax.all_gather(v_prompt, 'ctx', axis=0, tiled=True)  75.7 us
    all_gather x1, waiting for transfers between devices, body(): lax.all_gather(k_resp[0], 'ctx', axis=0, tiled=True)  75.1 us
    all_gather x1, waiting for transfers between devices, body(): lax.all_gather(k_prompt, 'ctx', axis=0, tiled=True)  73 us
    psum x1, blocking collectives, body(): prompt_final = lax.psum(prompt_share, 'resp').astype(jnp.bfloat16)  57.4 us
  transfers between devices with their start and end apart: 6, of which 6 were waited for; matrix products, arithmetic and copies ran while one was open for 5% of the time, Pallas kernels for 0%

commit v1 on v0

v1 whole, which is shorter than its diff:
```python
import functools
import math

import jax
import jax.numpy as jnp
from jax import lax
from jax.experimental import pallas as pl
from jax.experimental.pallas import tpu as pltpu
from jax.sharding import Mesh
from jax.sharding import PartitionSpec as P

HEADS = 16
KV_HEADS = 4
HEAD_DIM = 128
GROUP = HEADS // KV_HEADS
RESP_LEN = 2048
PROMPT_LEN = 1024
CTX = ("xh", "zh", "zl")
QUAD = ("xh", "zl")
ROWS = 128
PROWS = 64
CHUNK = 256
KEYS = PROMPT_LEN + RESP_LEN
PROMPT_CHUNKS = PROMPT_LEN // CHUNK
CHUNKS = KEYS // CHUNK
LANES = GROUP * ROWS
SCALE = HEAD_DIM**-0.5
SCALE2 = SCALE * math.log2(math.e)
NEG = -1e30
F32 = jnp.float32
BF16 = jnp.bfloat16


def dot(a, b):
    return jnp.dot(a, b, preferred_element_type=F32)


def attn_kernel(
    info,
    weight,
    qd,
    kv,
    od,
    dkv,
    k_s,
    v_s,
    kt_s,
    vt_s,
    score_s,
    prob_s,
    dk_s,
    dv_s,
    q_s,
    qt_s,
    upt_s,
    upl_s,
    uplt_s,
    acc_s,
):
    zh, length, count = info[0], info[1], info[2]
    up_weight = weight[0]

    def load_block(i, carry):
        at_p = pl.ds(pl.multiple_of(i * PROWS, PROWS), PROWS)
        at_r = pl.ds(pl.multiple_of(PROMPT_LEN + i * ROWS, ROWS), ROWS)
        k_s[at_r, :] = kv[i, :ROWS, :HEAD_DIM]
        v_s[at_r, :] = kv[i, :ROWS, HEAD_DIM:]
        k_s[at_p, :] = kv[i, ROWS:, :HEAD_DIM]
        v_s[at_p, :] = kv[i, ROWS:, HEAD_DIM:]
        return carry

    lax.fori_loop(0, 16, load_block, 0)

    def turn_chunk(c, carry):
        at = pl.ds(pl.multiple_of(c * CHUNK, CHUNK), CHUNK)
        kt_s[c] = k_s[at, :].T
        vt_s[c] = v_s[at, :].T
        dk_s[at, :] = jnp.zeros((CHUNK, HEAD_DIM), F32)
        dv_s[at, :] = jnp.zeros((CHUNK, HEAD_DIM), F32)
        return carry

    lax.fori_loop(0, CHUNKS, turn_chunk, 0)

    def tile(s, carry):
        block = (s // 2) * 8 + zh * 2 + s % 2
        row = block * ROWS + lax.broadcasted_iota(jnp.int32, (1, ROWS), 1)
        row_weight = jnp.where(row < count, up_weight, 0.0)
        row_valid = jnp.where(row < length, 1.0, 0.0)
        for h in range(GROUP):
            cols = slice(h * HEAD_DIM, (h + 1) * HEAD_DIM)
            q_head = qd[s, :, cols]
            q_s[cols, :] = q_head
            qt_s[:, cols] = q_head.T
            grad = qd[s, :, LANES + h * HEAD_DIM : LANES + (h + 1) * HEAD_DIM]
            upt_s[:, cols] = (grad.T.astype(F32) * row_weight).astype(BF16)
        last = PROMPT_CHUNKS + block // 2

        def score_step(c, running):
            at = pl.ds(pl.multiple_of(c * CHUNK, CHUNK), CHUNK)
            score = dot(k_s[at, :], qt_s[...])
            score_s[at, :] = score
            return jnp.maximum(running, jnp.max(score.reshape(CHUNK // 8, 8, LANES), axis=0))

        running = lax.fori_loop(0, last, score_step, jnp.full((8, LANES), NEG, F32))
        last_at = pl.ds(pl.multiple_of(last * CHUNK, CHUNK), CHUNK)
        score = dot(k_s[last_at, :], qt_s[...])
        key_row = (last - PROMPT_CHUNKS) * CHUNK + lax.broadcasted_iota(
            jnp.int32, (CHUNK, LANES), 0
        )
        query_row = block * ROWS + lax.broadcasted_iota(jnp.int32, (CHUNK, LANES), 1) % ROWS
        score = jnp.where(key_row <= query_row, score, NEG)
        score_s[last_at, :] = score
        running = jnp.maximum(running, jnp.max(score.reshape(CHUNK // 8, 8, LANES), axis=0))
        shift = jnp.max(running, axis=0, keepdims=True) * SCALE2

        acc_s[...] = jnp.zeros_like(acc_s)

        def prob_step(c, total):
            at = pl.ds(pl.multiple_of(c * CHUNK, CHUNK), CHUNK)
            prob = jnp.exp2(score_s[at, :] * SCALE2 - shift)
            low = prob.astype(BF16)
            prob_s[at, :] = low
            acc_s[...] += dot(vt_s[c], low)
            return total + jnp.sum(prob.reshape(CHUNK // 8, 8, LANES), axis=0)

        total = lax.fori_loop(0, last + 1, prob_step, jnp.zeros((8, LANES), F32))
        inverse = 1.0 / jnp.sum(total, axis=0, keepdims=True)
        valid = jnp.concatenate([row_valid] * GROUP, axis=1)
        out_t = (acc_s[...] * (inverse * valid)).astype(BF16)
        up_low = (upt_s[...].astype(F32) * inverse).astype(BF16)
        uplt_s[...] = up_low
        delta = jnp.sum(up_low.astype(F32) * out_t.astype(F32), axis=0, keepdims=True)
        for h in range(GROUP):
            cols = slice(h * HEAD_DIM, (h + 1) * HEAD_DIM)
            od[s, :, cols] = out_t[:, cols].T
            upl_s[cols, :] = up_low[:, cols].T

        acc_s[...] = jnp.zeros_like(acc_s)

        def back_step(c, carry):
            at = pl.ds(pl.multiple_of(c * CHUNK, CHUNK), CHUNK)
            low = prob_s[at, :]
            prob_grad = dot(v_s[at, :], uplt_s[...])
            score_grad = (low.astype(F32) * (prob_grad - delta)).astype(BF16)
            dv_s[at, :] += dot(low, upl_s[...])
            dk_s[at, :] += dot(score_grad, q_s[...])
            acc_s[...] += dot(kt_s[c], score_grad)
            return carry

        lax.fori_loop(0, last + 1, back_step, 0)
        dq_t = (acc_s[...] * SCALE).astype(BF16)
        for h in range(GROUP):
            cols = slice(h * HEAD_DIM, (h + 1) * HEAD_DIM)
            od[s, :, LANES + h * HEAD_DIM : LANES + (h + 1) * HEAD_DIM] = dq_t[:, cols].T
        return carry

    lax.fori_loop(0, 4, tile, 0)

    def store_block(i, carry):
        at_p = pl.ds(pl.multiple_of(i * PROWS, PROWS), PROWS)
        at_r = pl.ds(pl.multiple_of(PROMPT_LEN + i * ROWS, ROWS), ROWS)
        dkv[i, :ROWS, :HEAD_DIM] = (dk_s[at_r, :] * SCALE).astype(BF16)
        dkv[i, :ROWS, HEAD_DIM:] = dv_s[at_r, :].astype(BF16)
        dkv[i, ROWS:, :HEAD_DIM] = (dk_s[at_p, :] * SCALE).astype(BF16)
        dkv[i, ROWS:, HEAD_DIM:] = dv_s[at_p, :].astype(BF16)
        return carry

    lax.fori_loop(0, 16, store_block, 0)


def attend(info, weight, qd, kv):
    vmem = pl.BlockSpec(memory_space=pltpu.VMEM)
    smem = pl.BlockSpec(memory_space=pltpu.SMEM)
    return pl.pallas_call(
        attn_kernel,
        out_shape=(
            jax.ShapeDtypeStruct(qd.shape, BF16),
            jax.ShapeDtypeStruct(kv.shape, BF16),
        ),
        in_specs=[smem, smem, vmem, vmem],
        out_specs=(vmem, vmem),
        scratch_shapes=[
            pltpu.VMEM((KEYS, HEAD_DIM), BF16),
            pltpu.VMEM((KEYS, HEAD_DIM), BF16),
            pltpu.VMEM((CHUNKS, HEAD_DIM, CHUNK), BF16),
            pltpu.VMEM((CHUNKS, HEAD_DIM, CHUNK), BF16),
            pltpu.VMEM((KEYS, LANES), F32),
            pltpu.VMEM((KEYS, LANES), BF16),
            pltpu.VMEM((KEYS, HEAD_DIM), F32),
            pltpu.VMEM((KEYS, HEAD_DIM), F32),
            pltpu.VMEM((LANES, HEAD_DIM), BF16),
            pltpu.VMEM((HEAD_DIM, LANES), BF16),
            pltpu.VMEM((HEAD_DIM, LANES), BF16),
            pltpu.VMEM((LANES, HEAD_DIM), BF16),
            pltpu.VMEM((HEAD_DIM, LANES), BF16),
            pltpu.VMEM((HEAD_DIM, LANES), F32),
        ],
        compiler_params=pltpu.CompilerParams(vmem_limit_bytes=48 * 1024 * 1024),
        cost_estimate=pl.CostEstimate(
            flops=8_000_000_000, bytes_accessed=6_000_000, transcendentals=5_000_000
        ),
    )(info, weight, qd, kv)


def heads_first(x):
    rows = x.shape[0]
    return x.reshape(rows, KV_HEADS, -1).transpose(1, 0, 2)


def body(q_resp, k_resp, v_resp, k_prompt, v_prompt, d_out, lengths, counts):
    zh = lax.axis_index("zh").astype(jnp.int32)
    qd = jnp.concatenate([heads_first(q_resp[0]), heads_first(d_out[0])], axis=2)
    keys = jnp.concatenate([k_resp[0], k_prompt], axis=0)
    values = jnp.concatenate([v_resp[0], v_prompt], axis=0)
    kv = jnp.concatenate([heads_first(keys), heads_first(values)], axis=2)
    rows = ROWS + PROWS
    kv = jnp.broadcast_to(
        kv.reshape(2, 1, 2, rows, 2 * HEAD_DIM), (2, 4, 2, rows, 2 * HEAD_DIM)
    ).reshape(16, rows, 2 * HEAD_DIM)
    kv = lax.all_to_all(kv, CTX, 0, 0, tiled=True)
    qd = lax.all_to_all(qd, QUAD, 0, 0, tiled=True)
    info = jnp.stack([zh, lengths[0], counts[0]])
    weight = (RESP_LEN / counts[0].astype(F32)).reshape(1)
    od, dkv = attend(info, weight, qd, kv)
    dkv = lax.all_to_all(dkv, CTX, 0, 0, tiled=True)
    od = lax.all_to_all(od, QUAD, 0, 0, tiled=True)

    def whole(x):
        return x.transpose(1, 0, 2).reshape(x.shape[1], -1)

    attended = whole(od[:, :, :LANES])
    query_grad = whole(od[:, :, LANES:])
    dkv = jnp.sum(dkv.reshape(2, 4, 2, rows, 2 * HEAD_DIM).astype(F32), axis=1)
    dkv = dkv.astype(BF16).reshape(KV_HEADS, rows, 2 * HEAD_DIM)
    key_grad = whole(dkv[:, :ROWS, :HEAD_DIM])
    value_grad = whole(dkv[:, :ROWS, HEAD_DIM:])
    share = dkv[:, ROWS:].reshape(KV_HEADS, 16, PROWS // 16, 2 * HEAD_DIM).transpose(1, 0, 2, 3)
    share = share.reshape(16, 4 * PROWS // 16 * 2, HEAD_DIM)
    share = lax.all_to_all(share, "resp", 0, 0, tiled=True)
    share = jnp.sum(share.astype(F32), axis=0, keepdims=True).astype(BF16)
    share = jnp.broadcast_to(share, (16,) + share.shape[1:])
    share = lax.all_to_all(share, "resp", 0, 0, tiled=True)
    share = share.reshape(16, KV_HEADS, PROWS // 16, 2, HEAD_DIM).transpose(3, 0, 2, 1, 4)
    share = share.reshape(2, PROWS, KV_HEADS * HEAD_DIM)
    return (
        attended[None],
        query_grad[None],
        key_grad[None],
        value_grad[None],
        share[0],
        share[1],
    )


def solution(mesh):
    split = Mesh(mesh.devices.reshape(2, 4, 2, 16), ("xh", "zh", "zl", "resp"))
    return jax.shard_map(
        body,
        mesh=split,
        in_specs=(
            P("resp", CTX, None),
            P("resp", CTX, None),
            P("resp", CTX, None),
            P(CTX, None),
            P(CTX, None),
            P("resp", CTX, None),
            P("resp"),
            P("resp"),
        ),
        out_specs=(
            P("resp", CTX, None),
            P("resp", CTX, None),
            P("resp", CTX, None),
            P("resp", CTX, None),
            P(CTX, None),
            P(CTX, None),
        ),
        check_vma=False,
    )
```

time: 839 us -> 195 us (0.23)
  waiting for transfers between devices: 670 us -> 71 us
  local copies, waits for them, and re-layouts: 59.1 us -> 10.9 us
  starting transfers between devices: 0.24 us -> 28.7 us
  Pallas kernels: 0 us -> 27.4 us
  matrix products: 20.1 us -> 0 us
  between operations: 15.6 us -> 2.2 us
  other arithmetic: 10.6 us -> 2.08 us
    reduce_scatter x2 -> x0, waiting for transfers between devices: 360 us -> none  [the longest x1 192 us: body(): lax.psum_scatter(prompt_buf, 'ctx', scatter_dimension=0, tiled=True)]
    all_gather x4 -> x0, waiting for transfers between devices: 308 us -> none  [the longest x1 84.5 us: body(): lax.all_gather(v_resp[0], 'ctx', axis=0, tiled=True)]
    all_to_all x0 -> x5, waiting for transfers between devices: none -> 71 us  [the longest x1 35.7 us: body(): kv = lax.all_to_all(kv, CTX, 0, 0, tiled=True)]
    psum x1 -> x0, blocking collectives: 57.4 us -> none  [body(): prompt_final = lax.psum(prompt_share, 'resp').astype(jnp.bfloat16)]
    all_to_all x0 -> x1, blocking collectives: none -> 52.2 us  [body(): dkv = lax.all_to_all(dkv, CTX, 0, 0, tiled=True)]
    all_to_all x0 -> x5, starting transfers between devices: none -> 28.7 us  [the longest x2 9.88 us: body(): share = lax.all_to_all(share, 'resp', 0, 0, tiled=True)]
    pallas_call x0 -> x1, Pallas kernels: none -> 27.4 us  [attend(): pl.pallas_call(attn_kernel, out_shape=(jax.ShapeDtypeStruct(qd.shape, BF1...]
    dynamic_slice x12 -> x0, local copies, waits for them, and re-layouts: 25.3 us -> none  [the longest x6 15.3 us: backward_step(): current = lax.dynamic_slice_in_dim(buffer, key_start, block_size, 0)]
  transfers between devices with their start and end apart: 6 -> 5, of which waited for: 6 -> 5; matrix products, arithmetic and copies ran while one was open for 5% -> 3% of each run, Pallas kernels for 0% -> 0%
where the time goes in v1:
time: 195 us; the launch traced here: 194 us
  waiting for transfers between devices  71 us (36%)
  blocking collectives  52.2 us (27%)
  starting transfers between devices  28.7 us (15%)
  Pallas kernels  27.4 us (14%)
  local copies, waits for them, and re-layouts  10.9 us (6%)
  between operations  2.2 us (1%)
  other arithmetic  2.08 us (1%)
    all_to_all x1, blocking collectives, body(): dkv = lax.all_to_all(dkv, CTX, 0, 0, tiled=True)  52.2 us
    all_to_all x1, waiting for transfers between devices, body(): kv = lax.all_to_all(kv, CTX, 0, 0, tiled=True)  35.7 us
    pallas_call x1, Pallas kernels, attend(): pl.pallas_call(attn_kernel, out_shape=(jax.ShapeDtypeStruct(qd.shape, BF1...  27.4 us
    all_to_all x1, waiting for transfers between devices, body(): qd = lax.all_to_all(qd, QUAD, 0, 0, tiled=True)  13.9 us
    all_to_all x1, waiting for transfers between devices, body(): od = lax.all_to_all(od, QUAD, 0, 0, tiled=True)  13.3 us
    all_to_all x2, starting transfers between devices, body(): share = lax.all_to_all(share, 'resp', 0, 0, tiled=True)  9.88 us
    all_to_all x2, waiting for transfers between devices, body(): share = lax.all_to_all(share, 'resp', 0, 0, tiled=True)  8 us
    all_to_all x1, starting transfers between devices, body(): kv = lax.all_to_all(kv, CTX, 0, 0, tiled=True)  7.96 us
  transfers between devices with their start and end apart: 5, of which 5 were waited for; matrix products, arithmetic and copies ran while one was open for 3% of the time, Pallas kernels for 0%

profile of v1, /device:TPU:1, one launch (start us, length us, event | category | flops | bytes accessed | tf_op | source)
XLA Modules:
  0.0 194.4 jit_solution(4098667049825818862)
XLA Ops:
  0.6 1.4 copy.36
  2.0 0.2 copy.37
  2.2 0.3 copy.38
  2.5 0.2 copy.39
  2.8 1.1 pad_maximum_fusion
  3.9 6.3 %all-to-all-start = ((bf16[4,128,1024]{2,1,0:T(8,128)(2,1)}), bf16[4,128,1024]{2,1,0:T(8,128)(2,1)S(1)}, u32[]{:S(2)}, u32[]{:S(2)}) async-start(bf16[4,128,1024]{2,1,0:T(8,128)(2,1)} %pad_maximum_fusion), calls=%async_computation | async-start | bytes 2097152 | tf_op jit(solution)/shard_map/all_to_all | solution.py:221
  10.4 0.3 maximum_bitcast_fusion
  10.7 0.2 pad_maximum_fusion.1
  10.9 13.9 %all-to-all-done.qd = bf16[4,128,1024]{2,1,0:T(8,128)(2,1)S(1)} async-done(((bf16[4,128,1024]{2,1,0:T(8,128)(2,1)}), bf16[4,128,1024]{2,1,0:T(8,128)(2,1)S(1)}, u32[]{:S(2)}, u32[]{:S(2)}) %all-to-all-start) | async-done | bytes 1048608 | tf_op jit(solution)/shard_map/all_to_all | solution.py:221
  24.8 1.3 broadcast_in_dim.14
  26.2 8.0 %all-to-all-start.1 = ((bf16[16,192,256]{2,1,0:T(8,128)(2,1)}), bf16[16,192,256]{2,1,0:T(8,128)(2,1)S(1)}, u32[]{:S(2)}, u32[]{:S(2)}) async-start(bf16[16,192,256]{2,1,0:T(8,128)(2,1)} %bitcast.40), calls=%async_computation.1 | async-start | bytes 3145728 | tf_op jit(solution)/shard_map/all_to_all | solution.py:220
  35.5 35.7 %all-to-all-done.1.kv = bf16[16,192,256]{2,1,0:T(8,128)(2,1)S(1)} async-done(((bf16[16,192,256]{2,1,0:T(8,128)(2,1)}), bf16[16,192,256]{2,1,0:T(8,128)(2,1)S(1)}, u32[]{:S(2)}, u32[]{:S(2)}) %all-to-all-start.1) | async-done | bytes 1572896 | tf_op jit(solution)/shard_map/all_to_all | solution.py:220
  71.3 27.4 %shard_map.127 = (bf16[4,128,1024]{2,1,0:T(8,128)(2,1)S(1)}, bf16[16,192,256]{2,1,0:T(8,128)(2,1)S(1)}) custom-call(s32[3]{0:T(128)S(1)} %pad_add_fusion.info, f32[1]{0:T(128)S(6)} %div.4.weight, bf16[4,128,1024]{2,1,0:T(8,128)(2,1)S(1)} %all-to-all-done.qd, bf16[16,192,256]{2,1,0:T(8,128)(2,1)S(1)} %all-to-all-done.1.kv), custom_call_target="tpu_custom_call" | custom-call | flops 8000000000 | bytes 6000000 | tf_op jit(solution)/shard_map/pallas_call | solution.py:174
  98.7 52.2 %all_to_all.30 = bf16[16,192,256]{2,1,0:T(8,128)(2,1)S(1)} all-to-all(bf16[16,192,256]{2,1,0:T(8,128)(2,1)S(1)} %get-tuple-element.9), channel_id=1, replica_groups=mesh['xh'=2,'zh'=4,'zl'=2,'resp'=16] {'xh','zh','zl'}, dimensions={0} | all-to-all | bytes 3145728 | tf_op jit(solution)/shard_map/all_to_all | solution.py:225
  150.9 4.5 %all-to-all-start.2 = ((bf16[4,128,1024]{2,1,0:T(8,128)(2,1)}), bf16[4,128,1024]{2,1,0:T(8,128)(2,1)S(1)}, u32[]{:S(2)}, u32[]{:S(2)}) async-start(bf16[4,128,1024]{2,1,0:T(8,128)(2,1)} %copy-done), calls=%async_computation.2 | async-start | bytes 2097152 | tf_op jit(solution)/shard_map/all_to_all | solution.py:226
  155.4 0.4 reduce_sum.24
  155.8 0.1 copy.53
  156.0 0.7 reshape.58
  156.7 13.3 %all-to-all-done.2 = bf16[4,128,1024]{2,1,0:T(8,128)(2,1)S(1)} async-done(((bf16[4,128,1024]{2,1,0:T(8,128)(2,1)}), bf16[4,128,1024]{2,1,0:T(8,128)(2,1)S(1)}, u32[]{:S(2)}, u32[]{:S(2)}) %all-to-all-start.2) | async-done | bytes 1048608 | tf_op jit(solution)/shard_map/all_to_all | solution.py:226
  170.0 5.9 %all-to-all-start.4 = ((bf16[16,32,128]{2,1,0:T(8,128)(2,1)}), bf16[16,32,128]{2,1,0:T(8,128)(2,1)S(1)}, u32[]{:S(2)}, u32[]{:S(2)}) async-start(bf16[16,32,128]{2,1,0:T(8,128)(2,1)} %reshape.58), calls=%async_computation.4 | async-start | bytes 262144 | tf_op jit(solution)/shard_map/all_to_all | solution.py:239
  176.0 0.3 copy.42
  176.3 1.0 copy.51
  177.3 0.3 copy.41
  177.6 1.0 copy.50
  178.6 3.5 %all-to-all-done.4 = bf16[16,32,128]{2,1,0:T(8,128)(2,1)S(1)} async-done(((bf16[16,32,128]{2,1,0:T(8,128)(2,1)}), bf16[16,32,128]{2,1,0:T(8,128)(2,1)S(1)}, u32[]{:S(2)}, u32[]{:S(2)}) %all-to-all-start.4) | async-done | bytes 131104 | tf_op jit(solution)/shard_map/all_to_all | solution.py:239
  182.1 0.7 broadcast_in_dim.15
  182.8 4.0 %all-to-all-start.5 = ((bf16[16,32,128]{2,1,0:T(8,128)(2,1)}), bf16[16,32,128]{2,1,0:T(8,128)(2,1)S(1)}, u32[]{:S(2)}, u32[]{:S(2)}) async-start(bf16[16,32,128]{2,1,0:T(8,128)(2,1)} %broadcast_in_dim.15), calls=%async_computation.5 | async-start | bytes 262144 | tf_op jit(solution)/shard_map/all_to_all | solution.py:242
  186.9 0.7 broadcast_in_dim_reshape.15
  187.7 0.7 broadcast_in_dim_reshape.14
  188.4 4.5 %all-to-all-done.5 = bf16[16,32,128]{2,1,0:T(8,128)(2,1)S(1)} async-done(((bf16[16,32,128]{2,1,0:T(8,128)(2,1)}), bf16[16,32,128]{2,1,0:T(8,128)(2,1)S(1)}, u32[]{:S(2)}, u32[]{:S(2)}) %all-to-all-start.5) | async-done | bytes 131104 | tf_op jit(solution)/shard_map/all_to_all | solution.py:242
  193.1 0.6 copy.58
  193.8 0.6 copy.59
  (29 shorter events, 0.9 us)
Async XLA Ops:
  0.6 1.6 copy-start.1
  2.7 7.5 %copy-start.4 = (bf16[64,512]{1,0:T(8,128)(2,1)S(1)}, bf16[64,512]{1,0:T(8,128)(2,1)}, u32[]{:S(2)}) copy-start(bf16[64,512]{1,0:T(8,128)(2,1)} %param.11) | copy-start | bytes 196612
  3.9 6.4 %copy-start.5 = (bf16[64,512]{1,0:T(8,128)(2,1)S(1)}, bf16[64,512]{1,0:T(8,128)(2,1)}, u32[]{:S(2)}) copy-start(bf16[64,512]{1,0:T(8,128)(2,1)} %param.12) | copy-start | bytes 196612
  3.9 6.4 %copy-start.2 = (bf16[1,128,512]{2,1,0:T(8,128)(2,1)S(1)}, bf16[1,128,512]{2,1,0:T(8,128)(2,1)}, u32[]{:S(2)}) copy-start(bf16[1,128,512]{2,1,0:T(8,128)(2,1)} %param.9) | copy-start | bytes 393220
  3.9 6.4 %copy-start.3 = (bf16[1,128,512]{2,1,0:T(8,128)(2,1)S(1)}, bf16[1,128,512]{2,1,0:T(8,128)(2,1)}, u32[]{:S(2)}) copy-start(bf16[1,128,512]{2,1,0:T(8,128)(2,1)} %param.10) | copy-start | bytes 393220
  3.9 20.9 %all-to-all-start = ((bf16[4,128,1024]{2,1,0:T(8,128)(2,1)}), bf16[4,128,1024]{2,1,0:T(8,128)(2,1)S(1)}, u32[]{:S(2)}, u32[]{:S(2)}) async-start(bf16[4,128,1024]{2,1,0:T(8,128)(2,1)} %pad_maximum_fusion), calls=%async_computation | async-start | bytes 2097152 | tf_op jit(solution)/shard_map/all_to_all | solution.py:221
  26.2 45.1 %all-to-all-start.1 = ((bf16[16,192,256]{2,1,0:T(8,128)(2,1)}), bf16[16,192,256]{2,1,0:T(8,128)(2,1)S(1)}, u32[]{:S(2)}, u32[]{:S(2)}) async-start(bf16[16,192,256]{2,1,0:T(8,128)(2,1)} %bitcast.40), calls=%async_computation.1 | async-start | bytes 3145728 | tf_op jit(solution)/shard_map/all_to_all | solution.py:220
  98.7 52.2 %copy-start = (bf16[4,128,1024]{2,1,0:T(8,128)(2,1)}, bf16[4,128,1024]{2,1,0:T(8,128)(2,1)S(1)}, u32[]{:S(2)}) copy-start(bf16[4,128,1024]{2,1,0:T(8,128)(2,1)S(1)} %get-tuple-element.8) | copy-start | bytes 3145732
  150.9 19.1 %all-to-all-start.2 = ((bf16[4,128,1024]{2,1,0:T(8,128)(2,1)}), bf16[4,128,1024]{2,1,0:T(8,128)(2,1)S(1)}, u32[]{:S(2)}, u32[]{:S(2)}) async-start(bf16[4,128,1024]{2,1,0:T(8,128)(2,1)} %copy-done), calls=%async_computation.2 | async-start | bytes 2097152 | tf_op jit(solution)/shard_map/all_to_all | solution.py:226
  170.0 12.1 %all-to-all-start.4 = ((bf16[16,32,128]{2,1,0:T(8,128)(2,1)}), bf16[16,32,128]{2,1,0:T(8,128)(2,1)S(1)}, u32[]{:S(2)}, u32[]{:S(2)}) async-start(bf16[16,32,128]{2,1,0:T(8,128)(2,1)} %reshape.58), calls=%async_computation.4 | async-start | bytes 262144 | tf_op jit(solution)/shard_map/all_to_all | solution.py:239
  182.8 10.2 %all-to-all-start.5 = ((bf16[16,32,128]{2,1,0:T(8,128)(2,1)}), bf16[16,32,128]{2,1,0:T(8,128)(2,1)S(1)}, u32[]{:S(2)}, u32[]{:S(2)}) async-start(bf16[16,32,128]{2,1,0:T(8,128)(2,1)} %broadcast_in_dim.15), calls=%async_computation.5 | async-start | bytes 262144 | tf_op jit(solution)/shard_map/all_to_all | solution.py:242

commit v2 on v1

v2 whole, which is shorter than its diff:
```python
import math

import jax
import jax.numpy as jnp
from jax import lax
from jax.experimental import pallas as pl
from jax.experimental.pallas import tpu as pltpu
from jax.sharding import Mesh
from jax.sharding import PartitionSpec as P

HEADS = 16
KV_HEADS = 4
HEAD_DIM = 128
GROUP = HEADS // KV_HEADS
RESP_LEN = 2048
PROMPT_LEN = 1024
CTX = ("xh", "zh", "zl")
QUAD = ("xh", "zl")
RESP = ("y", "xl", "core")
ROWS = 128
PROWS = 64
BOTH = ROWS + PROWS
CHUNK = 512
KEYS = PROMPT_LEN + RESP_LEN
PROMPT_CHUNKS = PROMPT_LEN // CHUNK
CHUNKS = KEYS // CHUNK
HALF = GROUP * ROWS
LANES = 2 * HALF
SCALE = HEAD_DIM**-0.5
SCALE2 = SCALE * math.log2(math.e)
NEG = -1e30
F32 = jnp.float32
BF16 = jnp.bfloat16
VMEM = pl.BlockSpec(memory_space=pltpu.VMEM)
SMEM = pl.BlockSpec(memory_space=pltpu.SMEM)


def dot(a, b):
    return jnp.dot(a, b, preferred_element_type=F32)


def head_at(h, width=HEAD_DIM):
    return slice(h * width, (h + 1) * width)


def pack_kernel(info, q, do, k, v, kp, vp, qd0, qd1, qd2, qd3, kv):
    mine = info[0]
    for d, qd in enumerate((qd0, qd1, qd2, qd3)):
        at = pl.ds(pl.multiple_of((mine ^ d) * HALF, HALF), HALF)
        qd[:, :HALF] = q[:, at]
        qd[:, HALF:] = do[:, at]
    for h in range(KV_HEADS):
        for z in range(4):
            to = (h // 2) * 8 + z * 2 + h % 2
            kv[to, :ROWS, :HEAD_DIM] = k[:, head_at(h)]
            kv[to, :ROWS, HEAD_DIM:] = v[:, head_at(h)]
            kv[to, ROWS:, :HEAD_DIM] = kp[:, head_at(h)]
            kv[to, ROWS:, HEAD_DIM:] = vp[:, head_at(h)]


def attn_kernel(
    info,
    weight,
    qd0,
    qd1,
    qd2,
    qd3,
    kv,
    od0,
    od1,
    od2,
    od3,
    dkv,
    k_s,
    v_s,
    kt_s,
    vt_s,
    score_s,
    prob_s,
    dk_s,
    dv_s,
    q_s,
    qt_s,
    upt_s,
    upl_s,
    uplt_s,
    acc_s,
):
    mine, zh, length, count = info[0], info[1], info[2], info[3]
    up_weight = weight[0]

    def load_block(i, carry):
        at_p = pl.ds(pl.multiple_of(i * PROWS, PROWS), PROWS)
        at_r = pl.ds(pl.multiple_of(PROMPT_LEN + i * ROWS, ROWS), ROWS)
        k_s[at_r, :] = kv[i, :ROWS, :HEAD_DIM]
        v_s[at_r, :] = kv[i, :ROWS, HEAD_DIM:]
        k_s[at_p, :] = kv[i, ROWS:, :HEAD_DIM]
        v_s[at_p, :] = kv[i, ROWS:, HEAD_DIM:]
        return carry

    lax.fori_loop(0, 16, load_block, 0)

    def turn_chunk(c, carry):
        at = pl.ds(pl.multiple_of(c * CHUNK, CHUNK), CHUNK)
        kt_s[c] = k_s[at, :].T
        vt_s[c] = v_s[at, :].T
        dk_s[at, :] = jnp.zeros((CHUNK, HEAD_DIM), F32)
        dv_s[at, :] = jnp.zeros((CHUNK, HEAD_DIM), F32)
        return carry

    lax.fori_loop(0, CHUNKS, turn_chunk, 0)

    def tile(half, qds, ods):
        first = half * 8 + zh * 2
        valids = []
        for j in range(2):
            start = (first + ((mine & 1) ^ j)) * ROWS
            row = start + lax.broadcasted_iota(jnp.int32, (1, ROWS), 1)
            row_weight = jnp.where(row < count, up_weight, 0.0)
            valids += [jnp.where(row < length, 1.0, 0.0)] * GROUP
            for h in range(GROUP):
                cols = slice(j * HALF + h * HEAD_DIM, j * HALF + (h + 1) * HEAD_DIM)
                q_head = qds[j][:, head_at(h)]
                q_s[cols, :] = q_head
                qt_s[:, cols] = q_head.T
                grad = qds[j][:, HALF + h * HEAD_DIM : HALF + (h + 1) * HEAD_DIM]
                upt_s[:, cols] = (grad.T.astype(F32) * row_weight).astype(BF16)
        last = PROMPT_CHUNKS + first * ROWS // CHUNK

        def score_step(c, running):
            at = pl.ds(pl.multiple_of(c * CHUNK, CHUNK), CHUNK)
            score = dot(k_s[at, :], qt_s[...])
            score_s[at, :] = score
            return jnp.maximum(running, jnp.max(score.reshape(CHUNK // 8, 8, LANES), axis=0))

        running = lax.fori_loop(0, last, score_step, jnp.full((8, LANES), NEG, F32))
        last_at = pl.ds(pl.multiple_of(last * CHUNK, CHUNK), CHUNK)
        score = dot(k_s[last_at, :], qt_s[...])
        key_row = (last - PROMPT_CHUNKS) * CHUNK + lax.broadcasted_iota(
            jnp.int32, (CHUNK, LANES), 0
        )
        lane = lax.broadcasted_iota(jnp.int32, (CHUNK, LANES), 1)
        query_row = (first + ((mine & 1) ^ (lane // HALF))) * ROWS + lane % ROWS
        score = jnp.where(key_row <= query_row, score, NEG)
        score_s[last_at, :] = score
        running = jnp.maximum(running, jnp.max(score.reshape(CHUNK // 8, 8, LANES), axis=0))
        shift = jnp.max(running, axis=0, keepdims=True) * SCALE2

        acc_s[...] = jnp.zeros_like(acc_s)

        def prob_step(c, total):
            at = pl.ds(pl.multiple_of(c * CHUNK, CHUNK), CHUNK)
            prob = jnp.exp2(score_s[at, :] * SCALE2 - shift)
            low = prob.astype(BF16)
            prob_s[at, :] = low
            acc_s[...] += dot(vt_s[c], low)
            return total + jnp.sum(prob.reshape(CHUNK // 8, 8, LANES), axis=0)

        total = lax.fori_loop(0, last + 1, prob_step, jnp.zeros((8, LANES), F32))
        inverse = 1.0 / jnp.sum(total, axis=0, keepdims=True)
        valid = jnp.concatenate(valids, axis=1)
        out_t = (acc_s[...] * (inverse * valid)).astype(BF16)
        up_low = (upt_s[...].astype(F32) * inverse).astype(BF16)
        uplt_s[...] = up_low
        delta = jnp.sum(up_low.astype(F32) * out_t.astype(F32), axis=0, keepdims=True)
        for j in range(2):
            for h in range(GROUP):
                cols = slice(j * HALF + h * HEAD_DIM, j * HALF + (h + 1) * HEAD_DIM)
                ods[j][:, head_at(h)] = out_t[:, cols].T
                upl_s[cols, :] = up_low[:, cols].T

        acc_s[...] = jnp.zeros_like(acc_s)

        def back_step(c, carry):
            at = pl.ds(pl.multiple_of(c * CHUNK, CHUNK), CHUNK)
            low = prob_s[at, :]
            prob_grad = dot(v_s[at, :], uplt_s[...])
            score_grad = (low.astype(F32) * (prob_grad - delta)).astype(BF16)
            dv_s[at, :] += dot(low, upl_s[...])
            dk_s[at, :] += dot(score_grad, q_s[...])
            acc_s[...] += dot(kt_s[c], score_grad)
            return carry

        lax.fori_loop(0, last + 1, back_step, 0)
        dq_t = (acc_s[...] * SCALE).astype(BF16)
        for j in range(2):
            for h in range(GROUP):
                cols = slice(j * HALF + h * HEAD_DIM, j * HALF + (h + 1) * HEAD_DIM)
                ods[j][:, HALF + h * HEAD_DIM : HALF + (h + 1) * HEAD_DIM] = dq_t[:, cols].T

    tile(mine // 2, (qd0, qd1), (od0, od1))
    tile(1 - mine // 2, (qd2, qd3), (od2, od3))

    def store_block(i, carry):
        at_p = pl.ds(pl.multiple_of(i * PROWS, PROWS), PROWS)
        at_r = pl.ds(pl.multiple_of(PROMPT_LEN + i * ROWS, ROWS), ROWS)
        dkv[i, :ROWS, :HEAD_DIM] = (dk_s[at_r, :] * SCALE).astype(BF16)
        dkv[i, :ROWS, HEAD_DIM:] = dv_s[at_r, :].astype(BF16)
        dkv[i, ROWS:, :HEAD_DIM] = (dk_s[at_p, :] * SCALE).astype(BF16)
        dkv[i, ROWS:, HEAD_DIM:] = dv_s[at_p, :].astype(BF16)
        return carry

    lax.fori_loop(0, 16, store_block, 0)


def unpack_kernel(info, od0, od1, od2, od3, attended, query_grad):
    mine = info[0]
    for d, od in enumerate((od0, od1, od2, od3)):
        at = pl.ds(pl.multiple_of((mine ^ d) * HALF, HALF), HALF)
        attended[:, at] = od[:, :HALF]
        query_grad[:, at] = od[:, HALF:]


def sum_kernel(dkv, key_grad, value_grad, share):
    for h in range(KV_HEADS):
        first = (h // 2) * 8 + h % 2
        both = dkv[first].astype(F32)
        for z in range(1, 4):
            both = both + dkv[first + 2 * z].astype(F32)
        both = both.astype(BF16)
        key_grad[:, head_at(h)] = both[:ROWS, :HEAD_DIM]
        value_grad[:, head_at(h)] = both[:ROWS, HEAD_DIM:]
        share[:, head_at(h)] = both[ROWS:, :HEAD_DIM]
        share[:, head_at(KV_HEADS + h)] = both[ROWS:, HEAD_DIM:]


def bf16(*shape):
    return jax.ShapeDtypeStruct(shape, BF16)


def attend(info, weight, *operands):
    return pl.pallas_call(
        attn_kernel,
        out_shape=(bf16(ROWS, LANES),) * 4 + (bf16(16, BOTH, 2 * HEAD_DIM),),
        in_specs=[SMEM, SMEM] + [VMEM] * 5,
        out_specs=(VMEM,) * 5,
        scratch_shapes=[
            pltpu.VMEM((KEYS, HEAD_DIM), BF16),
            pltpu.VMEM((KEYS, HEAD_DIM), BF16),
            pltpu.VMEM((CHUNKS, HEAD_DIM, CHUNK), BF16),
            pltpu.VMEM((CHUNKS, HEAD_DIM, CHUNK), BF16),
            pltpu.VMEM((KEYS, LANES), F32),
            pltpu.VMEM((KEYS, LANES), BF16),
            pltpu.VMEM((KEYS, HEAD_DIM), F32),
            pltpu.VMEM((KEYS, HEAD_DIM), F32),
            pltpu.VMEM((LANES, HEAD_DIM), BF16),
            pltpu.VMEM((HEAD_DIM, LANES), BF16),
            pltpu.VMEM((HEAD_DIM, LANES), BF16),
            pltpu.VMEM((LANES, HEAD_DIM), BF16),
            pltpu.VMEM((HEAD_DIM, LANES), BF16),
            pltpu.VMEM((HEAD_DIM, LANES), F32),
        ],
        compiler_params=pltpu.CompilerParams(vmem_limit_bytes=48 * 1024 * 1024),
        cost_estimate=pl.CostEstimate(
            flops=8_000_000_000, bytes_accessed=6_000_000, transcendentals=5_000_000
        ),
    )(info, weight, *operands)


def swap(x, axis):
    return lax.ppermute(x, axis, [(0, 1), (1, 0)])


def turn(x, axis, step):
    size = lax.axis_size(axis)
    return lax.ppermute(x, axis, [(i, (i + step) % size) for i in range(size)])


def partner(x, d):
    return lax.ppermute(x, QUAD, [(i, i ^ d) for i in range(4)])


def rounded(x):
    return lax.optimization_barrier(x.astype(BF16))


def body(q_resp, k_resp, v_resp, k_prompt, v_prompt, d_out, lengths, counts):
    mine = (lax.axis_index("xh") * 2 + lax.axis_index("zl")).astype(jnp.int32)
    zh = lax.axis_index("zh").astype(jnp.int32)
    info = jnp.stack([mine, zh, lengths[0], counts[0]])
    weight = (RESP_LEN / counts[0].astype(F32)).reshape(1)
    qd = pl.pallas_call(
        pack_kernel,
        out_shape=(bf16(ROWS, LANES),) * 4 + (bf16(16, BOTH, 2 * HEAD_DIM),),
        in_specs=[SMEM] + [VMEM] * 6,
        out_specs=(VMEM,) * 5,
    )(info, q_resp[0], d_out[0], k_resp[0], v_resp[0], k_prompt, v_prompt)
    qd, kv = list(qd[:4]), qd[4]
    for d in (3, 1, 2):
        qd[d] = partner(qd[d], d)
    kv = lax.all_to_all(kv, CTX, 0, 0, tiled=True)
    od = attend(info, weight, *qd, kv)
    od, dkv = list(od[:4]), od[4]
    for d in (3, 1, 2):
        od[d] = partner(od[d], d)
    dkv = lax.all_to_all(dkv, CTX, 0, 0, tiled=True)
    attended, query_grad = pl.pallas_call(
        unpack_kernel,
        out_shape=(bf16(ROWS, HEADS * HEAD_DIM),) * 2,
        in_specs=[SMEM] + [VMEM] * 4,
        out_specs=(VMEM,) * 2,
    )(info, *od)
    width = KV_HEADS * HEAD_DIM
    key_grad, value_grad, share = pl.pallas_call(
        sum_kernel,
        out_shape=(bf16(ROWS, width), bf16(ROWS, width), bf16(PROWS, 2 * width)),
        in_specs=[VMEM],
        out_specs=(VMEM,) * 3,
    )(dkv)
    for axis in ("core", "xl"):
        share = rounded(share.astype(F32) + swap(share, axis).astype(F32))
    across = share.astype(F32) + turn(share, "y", 2).astype(F32)
    beside = turn(share, "y", 1).astype(F32) + turn(share, "y", 3).astype(F32)
    share = (across + beside).astype(BF16)
    return (
        attended[None],
        query_grad[None],
        key_grad[None],
        value_grad[None],
        share[:, :width],
        share[:, width:],
    )


def solution(mesh):
    split = Mesh(mesh.devices.reshape(2, 4, 2, 4, 2, 2), CTX + RESP)
    rows = P(RESP, CTX, None)
    prompt = P(CTX, None)
    return jax.shard_map(
        body,
        mesh=split,
        in_specs=(rows, rows, rows, prompt, prompt, rows, P(RESP), P(RESP)),
        out_specs=(rows, rows, rows, rows, prompt, prompt),
        check_vma=False,
    )
```

time: 195 us -> 163 us (0.84)
  waiting for transfers between devices: 71 us -> 50.5 us
  local copies, waits for them, and re-layouts: 10.9 us -> 2.09 us
  blocking collectives: 52.2 us -> 48.1 us
    ppermute x0 -> x11, waiting for transfers between devices: none -> 50.5 us  [the longest x6 49 us: partner(): return lax.ppermute(x, QUAD, [(i, i ^ d) for i in range(4)])]
    all_to_all x1, waiting for transfers between devices: 35.7 us -> 0.01 us  [body(): kv = lax.all_to_all(kv, CTX, 0, 0, tiled=True)]
    all_to_all x4 -> x0, waiting for transfers between devices: 35.2 us -> none  [the longest x1 13.9 us: body(): qd = lax.all_to_all(qd, QUAD, 0, 0, tiled=True)]
    all_to_all x4 -> x0, starting transfers between devices: 20.7 us -> none  [the longest x2 9.88 us: body(): share = lax.all_to_all(share, 'resp', 0, 0, tiled=True)]
    ppermute x0 -> x11, starting transfers between devices: none -> 17.6 us  [the longest x6 8.39 us: partner(): return lax.ppermute(x, QUAD, [(i, i ^ d) for i in range(4)])]
    all_to_all x1, blocking collectives: 52.2 us -> 48.1 us  [body(): dkv = lax.all_to_all(dkv, CTX, 0, 0, tiled=True)]
    all_to_all x1, starting transfers between devices: 7.96 us -> 11.7 us  [body(): kv = lax.all_to_all(kv, CTX, 0, 0, tiled=True)]
    unnamed x19 -> x18, local copies, waits for them, and re-layouts: 5.08 us -> 1.43 us
  transfers between devices with their start and end apart: 5 -> 12, of which waited for: 5 -> 5; matrix products, arithmetic and copies ran while one was open for 3% -> 0% of each run, Pallas kernels for 0% -> 1%
where the time goes in v2:
time: 163 us; the launch traced here: 161 us
  waiting for transfers between devices  50.5 us (31%)
  blocking collectives  48.1 us (30%)
  starting transfers between devices  29.3 us (18%)
  Pallas kernels  27.4 us (17%)
  local copies, waits for them, and re-layouts  2.09 us (1%)
  between operations  2.08 us (1%)
  other arithmetic  1.66 us (1%)
    ppermute x6, waiting for transfers between devices, partner(): return lax.ppermute(x, QUAD, [(i, i ^ d) for i in range(4)])  49 us
    all_to_all x1, blocking collectives, body(): dkv = lax.all_to_all(dkv, CTX, 0, 0, tiled=True)  48.1 us
    pallas_call x1, Pallas kernels, attend(): pl.pallas_call(attn_kernel, out_shape=(bf16(ROWS, LANES),) * 4 + (bf16(16...  20 us
    all_to_all x1, starting transfers between devices, body(): kv = lax.all_to_all(kv, CTX, 0, 0, tiled=True)  11.7 us
    ppermute x6, starting transfers between devices, partner(): return lax.ppermute(x, QUAD, [(i, i ^ d) for i in range(4)])  8.39 us
    ppermute x3, starting transfers between devices, turn(): return lax.ppermute(x, axis, [(i, (i + step) % size) for i in range(size)])  5.68 us
    ppermute x2, starting transfers between devices, swap(): return lax.ppermute(x, axis, [(0, 1), (1, 0)])  3.52 us
  transfers between devices with their start and end apart: 12, of which 5 were waited for; matrix products, arithmetic and copies ran while one was open for 0% of the time, Pallas kernels for 1%

profile of v2, /device:TPU:1, one launch (start us, length us, event | category | flops | bytes accessed | tf_op | source)
XLA Modules:
  0.0 161.2 jit_solution(16590183264710580974)
XLA Ops:
  1.9 0.6 pad_add_fusion.info
  2.5 2.9 %shard_map.127 = (bf16[128,1024]{1,0:T(8,128)(2,1)}, bf16[128,1024]{1,0:T(8,128)(2,1)}, bf16[128,1024]{1,0:T(8,128)(2,1)}, bf16[128,1024]{1,0:T(8,128)(2,1)}, bf16[16,192,256]{2,1,0:T(8,128)(2,1)}) custom-call(s32[4]{0:T(128)} %pad_add_fusion.info, bf16[128,2048]{1,0:T(8,128)(2,1)} %bitcast.10, bf16[128,2048]{1,0:T(8,128)(2,1)} %bitcast.11, ...), custom_call_target="tpu_custom_call" | custom-call | tf_op jit(solution)/shard_map/pallas_call | solution.py:282
  5.5 0.0 copy-start.2
  5.5 11.7 %all-to-all-start = ((bf16[16,192,256]{2,1,0:T(8,128)(2,1)}), bf16[16,192,256]{2,1,0:T(8,128)(2,1)S(1)}, u32[]{:S(2)}, u32[]{:S(2)}) async-start(bf16[16,192,256]{2,1,0:T(8,128)(2,1)} %get-tuple-element.25), calls=%async_computation | async-start | bytes 3145728 | tf_op jit(solution)/shard_map/all_to_all | solution.py:291
  17.2 1.4 collective-permute-start
  18.7 2.7 %collective-permute-start.1 = (bf16[128,1024]{1,0:T(8,128)(2,1)S(1)}, bf16[128,1024]{1,0:T(8,128)(2,1)S(1)}, u32[]{:S(2)}, u32[]{:S(2)}) collective-permute-start(bf16[128,1024]{1,0:T(8,128)(2,1)S(1)} %copy-done.7), channel_id=1, source_target_pairs={{0,128},{16,144},{128,0},{144,16},{1,129},{17,145},{129,1},{145,17... | collective-permute-start | bytes 786440 | tf_op jit(solution)/shard_map/ppermute | solution.py:270
  21.4 0.1 collective-permute-start.2
  21.5 36.8 %collective-permute-done.qd1 = bf16[128,1024]{1,0:T(8,128)(2,1)S(1)} collective-permute-done((bf16[128,1024]{1,0:T(8,128)(2,1)S(1)}, bf16[128,1024]{1,0:T(8,128)(2,1)S(1)}, u32[]{:S(2)}, u32[]{:S(2)}) %collective-permute-start) | collective-permute-done | bytes 262176 | tf_op jit(solution)/shard_map/ppermute | solution.py:270
  58.3 0.0 collective-permute-done.1.qd2
  58.3 8.0 %collective-permute-done.2.qd3 = bf16[128,1024]{1,0:T(8,128)(2,1)S(1)} collective-permute-done((bf16[128,1024]{1,0:T(8,128)(2,1)S(1)}, bf16[128,1024]{1,0:T(8,128)(2,1)S(1)}, u32[]{:S(2)}, u32[]{:S(2)}) %collective-permute-start.2) | collective-permute-done | bytes 262176 | tf_op jit(solution)/shard_map/ppermute | solution.py:270
  66.3 20.0 %shard_map.128 = (bf16[128,1024]{1,0:T(8,128)(2,1)S(1)}, bf16[128,1024]{1,0:T(8,128)(2,1)S(1)}, bf16[128,1024]{1,0:T(8,128)(2,1)S(1)}, bf16[128,1024]{1,0:T(8,128)(2,1)S(1)}, bf16[16,192,256]{2,1,0:T(8,128)(2,1)S(1)}) custom-call(s32[4]{0:T(128)S(1)} %copy-done.1, f32[1]{0:T(128)S(6)} %div.4.weight, bf16[128,1024]{1,0:T(8,128)(2,1)S(1)} %copy-done.2, ...), custom_call_target="tpu_custom_call" | custom-call | flops 8000000000 | bytes 6000000 | tf_op jit(solution)/shard_map/pallas_call | solution.py:232
  86.4 0.7 copy-done
  87.1 48.1 %all_to_all.10.dkv = bf16[16,192,256]{2,1,0:T(8,128)(2,1)} all-to-all(bf16[16,192,256]{2,1,0:T(8,128)(2,1)S(1)} %get-tuple-element.32), channel_id=1, replica_groups=mesh['xh'=2,'zh'=4,'zl'=2,'y'=4,'xl'=2,'core'=2] {'xh','zh','zl'}, dimensions={0} | all-to-all | bytes 3145728 | tf_op jit(solution)/shard_map/all_to_all | solution.py:296
  135.2 2.3 %shard_map.130 = (bf16[128,512]{1,0:T(8,128)(2,1)}, bf16[128,512]{1,0:T(8,128)(2,1)}, bf16[64,1024]{1,0:T(8,128)(2,1)}) custom-call(bf16[16,192,256]{2,1,0:T(8,128)(2,1)} %all_to_all.10.dkv), custom_call_target="tpu_custom_call" | custom-call | tf_op jit(solution)/shard_map/pallas_call | solution.py:304
  137.5 3.1 %collective-permute-start.6 = (bf16[64,1024]{1,0:T(8,128)(2,1)}, bf16[64,1024]{1,0:T(8,128)(2,1)S(1)}, u32[]{:S(2)}, u32[]{:S(2)}) collective-permute-start(bf16[64,1024]{1,0:T(8,128)(2,1)} %get-tuple-element.35), channel_id=1, source_target_pairs={{0,1},{1,0},{2,3},{3,2},{4,5},{5,4},{6,7},{7,6},{8,9},{9,8},{10,11... | collective-permute-start | bytes 393224 | tf_op jit(solution)/shard_map/ppermute | solution.py:261
  140.6 1.2 collective-permute-done.6
  141.8 0.9 add_convert_fusion.2
  142.7 0.4 collective-permute-start.7
  143.1 0.8 collective-permute-start.3
  143.9 2.1 %collective-permute-start.4 = (bf16[128,1024]{1,0:T(8,128)(2,1)S(1)}, bf16[128,1024]{1,0:T(8,128)(2,1)S(1)}, u32[]{:S(2)}, u32[]{:S(2)}) collective-permute-start(bf16[128,1024]{1,0:T(8,128)(2,1)S(1)} %get-tuple-element.28), channel_id=1, source_target_pairs={{0,128},{16,144},{128,0},{144,16},{1,129},{17,145},{129,1},{145,17... | collective-permute-start | bytes 786440 | tf_op jit(solution)/shard_map/ppermute | solution.py:270
  146.0 1.2 collective-permute-start.5
  147.3 0.3 collective-permute-done.7
  147.6 2.8 %collective-permute-start.10 = (bf16[64,1024]{1,0:T(8,128)(2,1)S(1)}, bf16[64,1024]{1,0:T(8,128)(2,1)S(1)}, u32[]{:S(2)}, u32[]{:S(2)}) collective-permute-start(bf16[64,1024]{1,0:T(8,128)(2,1)S(1)} %add_convert_fusion.1), channel_id=1, source_target_pairs={{0,12},{4,0},{8,4},{12,8},{1,13},{5,1},{9,5},{13,9},{2,14},{6,2},{... | collective-permute-start | bytes 393224 | tf_op jit(solution)/shard_map/ppermute | solution.py:266
  150.4 2.9 %collective-permute-start.8 = (bf16[64,1024]{1,0:T(8,128)(2,1)S(1)}, bf16[64,1024]{1,0:T(8,128)(2,1)S(1)}, u32[]{:S(2)}, u32[]{:S(2)}) collective-permute-start(bf16[64,1024]{1,0:T(8,128)(2,1)S(1)} %add_convert_fusion.1), channel_id=1, source_target_pairs={{0,8},{4,12},{8,0},{12,4},{1,9},{5,13},{9,1},{13,5},{2,10},{6,14},... | collective-permute-start | bytes 393224 | tf_op jit(solution)/shard_map/ppermute | solution.py:266
  153.3 0.0 collective-permute-done.4.od2
  153.3 4.2 %collective-permute-done.5.od3 = bf16[128,1024]{1,0:T(8,128)(2,1)S(1)} collective-permute-done((bf16[128,1024]{1,0:T(8,128)(2,1)S(1)}, bf16[128,1024]{1,0:T(8,128)(2,1)S(1)}, u32[]{:S(2)}, u32[]{:S(2)}) %collective-permute-start.5) | collective-permute-done | bytes 262176 | tf_op jit(solution)/shard_map/ppermute | solution.py:270
  157.5 0.7 copy-done.5
  158.2 2.2 %shard_map.129 = (bf16[128,2048]{1,0:T(8,128)(2,1)}, bf16[128,2048]{1,0:T(8,128)(2,1)}) custom-call(s32[4]{0:T(128)} %pad_add_fusion.info, bf16[128,1024]{1,0:T(8,128)(2,1)} %copy-done, bf16[128,1024]{1,0:T(8,128)(2,1)} %copy-done.3, bf16[128,1024]{1,0:T(8,128)(2,1)} %copy-done.4, bf16[128,1024]{1,0:T(8,128)(2,1)} %copy-done.5), custom_call_target="tpu_custom_call" | custom-call | tf_op jit(solution)/shard_map/pallas_call | solution.py:297
  160.4 0.0 collective-permute-done.10
  160.4 0.0 collective-permute-done.9
  160.4 0.1 add_convert_fusion
  160.5 0.7 fusion
  (20 shorter events, 0.1 us)
Async XLA Ops:
  5.5 11.8 %copy-start.8 = (bf16[128,1024]{1,0:T(8,128)(2,1)S(1)}, bf16[128,1024]{1,0:T(8,128)(2,1)}, u32[]{:S(2)}) copy-start(bf16[128,1024]{1,0:T(8,128)(2,1)} %get-tuple-element.22) | copy-start | bytes 786436
  5.5 13.2 %copy-start.7 = (bf16[128,1024]{1,0:T(8,128)(2,1)S(1)}, bf16[128,1024]{1,0:T(8,128)(2,1)}, u32[]{:S(2)}) copy-start(bf16[128,1024]{1,0:T(8,128)(2,1)} %get-tuple-element.23) | copy-start | bytes 786436
  5.5 15.9 %copy-start.6 = (bf16[128,1024]{1,0:T(8,128)(2,1)S(1)}, bf16[128,1024]{1,0:T(8,128)(2,1)}, u32[]{:S(2)}) copy-start(bf16[128,1024]{1,0:T(8,128)(2,1)} %get-tuple-element.24) | copy-start | bytes 786436
  5.5 60.9 %copy-start.1 = (s32[4]{0:T(128)S(1)}, s32[4]{0:T(128)}, u32[]{:S(2)}) copy-start(s32[4]{0:T(128)} %pad_add_fusion.info) | copy-start | bytes 52
  5.5 60.9 %copy-start.2 = (bf16[128,1024]{1,0:T(8,128)(2,1)S(1)}, bf16[128,1024]{1,0:T(8,128)(2,1)}, u32[]{:S(2)}) copy-start(bf16[128,1024]{1,0:T(8,128)(2,1)} %get-tuple-element.21.qd0) | copy-start | bytes 786436
  5.5 60.8 %all-to-all-start = ((bf16[16,192,256]{2,1,0:T(8,128)(2,1)}), bf16[16,192,256]{2,1,0:T(8,128)(2,1)S(1)}, u32[]{:S(2)}, u32[]{:S(2)}) async-start(bf16[16,192,256]{2,1,0:T(8,128)(2,1)} %get-tuple-element.25), calls=%async_computation | async-start | bytes 3145728 | tf_op jit(solution)/shard_map/all_to_all | solution.py:291
  17.2 41.1 %collective-permute-start = (bf16[128,1024]{1,0:T(8,128)(2,1)S(1)}, bf16[128,1024]{1,0:T(8,128)(2,1)S(1)}, u32[]{:S(2)}, u32[]{:S(2)}) collective-permute-start(bf16[128,1024]{1,0:T(8,128)(2,1)S(1)} %copy-done.8), channel_id=1, source_target_pairs={{0,16},{16,0},{128,144},{144,128},{1,17},{17,1},{129,145},{145,129... | collective-permute-start | bytes 786440 | tf_op jit(solution)/shard_map/ppermute | solution.py:270
  18.7 39.6 %collective-permute-start.1 = (bf16[128,1024]{1,0:T(8,128)(2,1)S(1)}, bf16[128,1024]{1,0:T(8,128)(2,1)S(1)}, u32[]{:S(2)}, u32[]{:S(2)}) collective-permute-start(bf16[128,1024]{1,0:T(8,128)(2,1)S(1)} %copy-done.7), channel_id=1, source_target_pairs={{0,128},{16,144},{128,0},{144,16},{1,129},{17,145},{129,1},{145,17... | collective-permute-start | bytes 786440 | tf_op jit(solution)/shard_map/ppermute | solution.py:270
  21.4 44.9 %collective-permute-start.2 = (bf16[128,1024]{1,0:T(8,128)(2,1)S(1)}, bf16[128,1024]{1,0:T(8,128)(2,1)S(1)}, u32[]{:S(2)}, u32[]{:S(2)}) collective-permute-start(bf16[128,1024]{1,0:T(8,128)(2,1)S(1)} %copy-done.6), channel_id=1, source_target_pairs={{0,144},{16,128},{128,16},{144,0},{1,145},{17,129},{129,17},{145,1... | collective-permute-start | bytes 786440 | tf_op jit(solution)/shard_map/ppermute | solution.py:270
  86.3 0.7 copy-start
  137.5 4.3 %collective-permute-start.6 = (bf16[64,1024]{1,0:T(8,128)(2,1)}, bf16[64,1024]{1,0:T(8,128)(2,1)S(1)}, u32[]{:S(2)}, u32[]{:S(2)}) collective-permute-start(bf16[64,1024]{1,0:T(8,128)(2,1)} %get-tuple-element.35), channel_id=1, source_target_pairs={{0,1},{1,0},{2,3},{3,2},{4,5},{5,4},{6,7},{7,6},{8,9},{9,8},{10,11... | collective-permute-start | bytes 393224 | tf_op jit(solution)/shard_map/ppermute | solution.py:261
  142.7 4.8 %collective-permute-start.7 = (bf16[64,1024]{1,0:T(8,128)(2,1)S(1)}, bf16[64,1024]{1,0:T(8,128)(2,1)S(1)}, u32[]{:S(2)}, u32[]{:S(2)}) collective-permute-start(bf16[64,1024]{1,0:T(8,128)(2,1)S(1)} %add_convert_fusion.2), channel_id=1, source_target_pairs={{0,2},{2,0},{1,3},{3,1},{4,6},{6,4},{5,7},{7,5},{8,10},{10,8},{9,1... | collective-permute-start | bytes 393224 | tf_op jit(solution)/shard_map/ppermute | solution.py:261
  143.1 7.3 %collective-permute-start.3 = (bf16[128,1024]{1,0:T(8,128)(2,1)S(1)}, bf16[128,1024]{1,0:T(8,128)(2,1)S(1)}, u32[]{:S(2)}, u32[]{:S(2)}) collective-permute-start(bf16[128,1024]{1,0:T(8,128)(2,1)S(1)} %get-tuple-element.27), channel_id=1, source_target_pairs={{0,16},{16,0},{128,144},{144,128},{1,17},{17,1},{129,145},{145,129... | collective-permute-start | bytes 786440 | tf_op jit(solution)/shard_map/ppermute | solution.py:270
  143.9 9.3 %collective-permute-start.4 = (bf16[128,1024]{1,0:T(8,128)(2,1)S(1)}, bf16[128,1024]{1,0:T(8,128)(2,1)S(1)}, u32[]{:S(2)}, u32[]{:S(2)}) collective-permute-start(bf16[128,1024]{1,0:T(8,128)(2,1)S(1)} %get-tuple-element.28), channel_id=1, source_target_pairs={{0,128},{16,144},{128,0},{144,16},{1,129},{17,145},{129,1},{145,17... | collective-permute-start | bytes 786440 | tf_op jit(solution)/shard_map/ppermute | solution.py:270
  146.0 11.4 %collective-permute-start.5 = (bf16[128,1024]{1,0:T(8,128)(2,1)S(1)}, bf16[128,1024]{1,0:T(8,128)(2,1)S(1)}, u32[]{:S(2)}, u32[]{:S(2)}) collective-permute-start(bf16[128,1024]{1,0:T(8,128)(2,1)S(1)} %get-tuple-element.29), channel_id=1, source_target_pairs={{0,144},{16,128},{128,16},{144,0},{1,145},{17,129},{129,17},{145,1... | collective-permute-start | bytes 786440 | tf_op jit(solution)/shard_map/ppermute | solution.py:270
  147.6 12.9 %collective-permute-start.10 = (bf16[64,1024]{1,0:T(8,128)(2,1)S(1)}, bf16[64,1024]{1,0:T(8,128)(2,1)S(1)}, u32[]{:S(2)}, u32[]{:S(2)}) collective-permute-start(bf16[64,1024]{1,0:T(8,128)(2,1)S(1)} %add_convert_fusion.1), channel_id=1, source_target_pairs={{0,12},{4,0},{8,4},{12,8},{1,13},{5,1},{9,5},{13,9},{2,14},{6,2},{... | collective-permute-start | bytes 393224 | tf_op jit(solution)/shard_map/ppermute | solution.py:266
  150.4 10.0 %collective-permute-start.9 = (bf16[64,1024]{1,0:T(8,128)(2,1)S(1)}, bf16[64,1024]{1,0:T(8,128)(2,1)S(1)}, u32[]{:S(2)}, u32[]{:S(2)}) collective-permute-start(bf16[64,1024]{1,0:T(8,128)(2,1)S(1)} %add_convert_fusion.1), channel_id=1, source_target_pairs={{0,4},{4,8},{8,12},{12,0},{1,5},{5,9},{9,13},{13,1},{2,6},{6,10},{... | collective-permute-start | bytes 393224 | tf_op jit(solution)/shard_map/ppermute | solution.py:266
  150.4 7.1 %copy-start.3 = (bf16[128,1024]{1,0:T(8,128)(2,1)}, bf16[128,1024]{1,0:T(8,128)(2,1)S(1)}, u32[]{:S(2)}) copy-start(bf16[128,1024]{1,0:T(8,128)(2,1)S(1)} %collective-permute-done.3.od1) | copy-start | bytes 786436
  150.4 10.0 %collective-permute-start.8 = (bf16[64,1024]{1,0:T(8,128)(2,1)S(1)}, bf16[64,1024]{1,0:T(8,128)(2,1)S(1)}, u32[]{:S(2)}, u32[]{:S(2)}) collective-permute-start(bf16[64,1024]{1,0:T(8,128)(2,1)S(1)} %add_convert_fusion.1), channel_id=1, source_target_pairs={{0,8},{4,12},{8,0},{12,4},{1,9},{5,13},{9,1},{13,5},{2,10},{6,14},... | collective-permute-start | bytes 393224 | tf_op jit(solution)/shard_map/ppermute | solution.py:266
  153.3 4.2 %copy-start.4 = (bf16[128,1024]{1,0:T(8,128)(2,1)}, bf16[128,1024]{1,0:T(8,128)(2,1)S(1)}, u32[]{:S(2)}) copy-start(bf16[128,1024]{1,0:T(8,128)(2,1)S(1)} %collective-permute-done.4.od2) | copy-start | bytes 786436
  157.5 0.7 copy-start.5

commit v3 on v2

--- a/solution.py
+++ b/solution.py
@@ -14,8 +14,8 @@
 GROUP = HEADS // KV_HEADS
 RESP_LEN = 2048
 PROMPT_LEN = 1024
-CTX = ("xh", "zh", "zl")
-QUAD = ("xh", "zl")
+CTX = ("xh", "z")
+LOCAL = ("xh", "z", "core")
 RESP = ("y", "xl", "core")
 ROWS = 128
 PROWS = 64
@@ -43,19 +43,21 @@
     return slice(h * width, (h + 1) * width)
 
 
-def pack_kernel(info, q, do, k, v, kp, vp, qd0, qd1, qd2, qd3, kv):
+def pack_kernel(info, q, do, k, v, kp, vp, qd0, qd1, qd2, qd3, kv0, kv1, kv2, kv3):
     mine = info[0]
-    for d, qd in enumerate((qd0, qd1, qd2, qd3)):
+    for d, (qd, kv) in enumerate(((qd0, kv0), (qd1, kv1), (qd2, kv2), (qd3, kv3))):
         at = pl.ds(pl.multiple_of((mine ^ d) * HALF, HALF), HALF)
         qd[:, :HALF] = q[:, at]
         qd[:, HALF:] = do[:, at]
-    for h in range(KV_HEADS):
-        for z in range(4):
-            to = (h // 2) * 8 + z * 2 + h % 2
-            kv[to, :ROWS, :HEAD_DIM] = k[:, head_at(h)]
-            kv[to, :ROWS, HEAD_DIM:] = v[:, head_at(h)]
-            kv[to, ROWS:, :HEAD_DIM] = kp[:, head_at(h)]
-            kv[to, ROWS:, HEAD_DIM:] = vp[:, head_at(h)]
+        at = pl.ds(pl.multiple_of((mine ^ d) * HEAD_DIM, HEAD_DIM), HEAD_DIM)
+        kv[:ROWS, :HEAD_DIM] = k[:, at]
+        kv[:ROWS, HEAD_DIM:] = v[:, at]
+        kv[ROWS:, :HEAD_DIM] = kp[:, at]
+        kv[ROWS:, HEAD_DIM:] = vp[:, at]
+
+
+def block_of(member, quad, core):
+    return (member // 2) * 8 + ((quad * 2 + (member & 1) + core) & 7)
 
 
 def attn_kernel(
@@ -65,7 +67,14 @@
     qd1,
     qd2,
     qd3,
-    kv,
+    kv0,
+    kv1,
+    kv2,
+    kv3,
+    kv_left,
+    kv_right,
+    kv_far0,
+    kv_far1,
     od0,
     od1,
     od2,
@@ -86,19 +95,23 @@
     uplt_s,
     acc_s,
 ):
-    mine, zh, length, count = info[0], info[1], info[2], info[3]
+    mine, quad, core, length, count = info[0], info[1], info[2], info[3], info[4]
     up_weight = weight[0]
 
-    def load_block(i, carry):
-        at_p = pl.ds(pl.multiple_of(i * PROWS, PROWS), PROWS)
-        at_r = pl.ds(pl.multiple_of(PROMPT_LEN + i * ROWS, ROWS), ROWS)
-        k_s[at_r, :] = kv[i, :ROWS, :HEAD_DIM]
-        v_s[at_r, :] = kv[i, :ROWS, HEAD_DIM:]
-        k_s[at_p, :] = kv[i, ROWS:, :HEAD_DIM]
-        v_s[at_p, :] = kv[i, ROWS:, HEAD_DIM:]
-        return carry
-
-    lax.fori_loop(0, 16, load_block, 0)
+    def load_block(kv, d, step):
+        block = block_of(mine ^ d, (quad + step) & 3, core)
+        at_p = pl.ds(pl.multiple_of(block * PROWS, PROWS), PROWS)
+        at_r = pl.ds(pl.multiple_of(PROMPT_LEN + block * ROWS, ROWS), ROWS)
+        k_s[at_r, :] = kv[:ROWS, :HEAD_DIM]
+        v_s[at_r, :] = kv[:ROWS, HEAD_DIM:]
+        k_s[at_p, :] = kv[ROWS:, :HEAD_DIM]
+        v_s[at_p, :] = kv[ROWS:, HEAD_DIM:]
+
+    for d, kv in enumerate((kv0, kv1, kv2, kv3)):
+        load_block(kv, d, 0)
+        load_block(kv_left.at[d], d, 3)
+        load_block(kv_right.at[d], d, 1)
+        load_block((kv_far0, kv_far1)[d // 2].at[d % 2], d, 2)
 
     def turn_chunk(c, carry):
         at = pl.ds(pl.multiple_of(c * CHUNK, CHUNK), CHUNK)
@@ -111,12 +124,16 @@
     lax.fori_loop(0, CHUNKS, turn_chunk, 0)
 
     def tile(half, qds, ods):
-        first = half * 8 + zh * 2
-        valids = []
+        place0 = (quad * 2 + core) & 7
+        place1 = (quad * 2 + core + 1) & 7
+        lowest = half * 8 + jnp.minimum(place0, place1)
+        highest = half * 8 + jnp.maximum(place0, place1)
+        valids, rows = [], []
         for j in range(2):
-            start = (first + ((mine & 1) ^ j)) * ROWS
+            start = block_of(half * 2 + ((mine & 1) ^ j), quad, core) * ROWS
             row = start + lax.broadcasted_iota(jnp.int32, (1, ROWS), 1)
             row_weight = jnp.where(row < count, up_weight, 0.0)
+            rows += [row] * GROUP
             valids += [jnp.where(row < length, 1.0, 0.0)] * GROUP
             for h in range(GROUP):
                 cols = slice(j * HALF + h * HEAD_DIM, j * HALF + (h + 1) * HEAD_DIM)
@@ -125,7 +142,8 @@
                 qt_s[:, cols] = q_head.T
                 grad = qds[j][:, HALF + h * HEAD_DIM : HALF + (h + 1) * HEAD_DIM]
                 upt_s[:, cols] = (grad.T.astype(F32) * row_weight).astype(BF16)
-        last = PROMPT_CHUNKS + first * ROWS // CHUNK
+        free = PROMPT_CHUNKS + lowest * ROWS // CHUNK
+        steps = PROMPT_CHUNKS + highest * ROWS // CHUNK + 1
 
         def score_step(c, running):
             at = pl.ds(pl.multiple_of(c * CHUNK, CHUNK), CHUNK)
@@ -133,17 +151,19 @@
             score_s[at, :] = score
             return jnp.maximum(running, jnp.max(score.reshape(CHUNK // 8, 8, LANES), axis=0))
 
-        running = lax.fori_loop(0, last, score_step, jnp.full((8, LANES), NEG, F32))
-        last_at = pl.ds(pl.multiple_of(last * CHUNK, CHUNK), CHUNK)
-        score = dot(k_s[last_at, :], qt_s[...])
-        key_row = (last - PROMPT_CHUNKS) * CHUNK + lax.broadcasted_iota(
-            jnp.int32, (CHUNK, LANES), 0
-        )
-        lane = lax.broadcasted_iota(jnp.int32, (CHUNK, LANES), 1)
-        query_row = (first + ((mine & 1) ^ (lane // HALF))) * ROWS + lane % ROWS
-        score = jnp.where(key_row <= query_row, score, NEG)
-        score_s[last_at, :] = score
-        running = jnp.maximum(running, jnp.max(score.reshape(CHUNK // 8, 8, LANES), axis=0))
+        def masked_step(c, running):
+            at = pl.ds(pl.multiple_of(c * CHUNK, CHUNK), CHUNK)
+            score = dot(k_s[at, :], qt_s[...])
+            key_row = (c - PROMPT_CHUNKS) * CHUNK + lax.broadcasted_iota(
+                jnp.int32, (CHUNK, LANES), 0
+            )
+            score = jnp.where(key_row <= query_row, score, NEG)
+            score_s[at, :] = score
+            return jnp.maximum(running, jnp.max(score.reshape(CHUNK // 8, 8, LANES), axis=0))
+
+        query_row = jnp.concatenate(rows, axis=1)
+        running = lax.fori_loop(0, free, score_step, jnp.full((8, LANES), NEG, F32))
+        running = lax.fori_loop(free, steps, masked_step, running)
         shift = jnp.max(running, axis=0, keepdims=True) * SCALE2
 
         acc_s[...] = jnp.zeros_like(acc_s)
@@ -156,7 +176,7 @@
             acc_s[...] += dot(vt_s[c], low)
             return total + jnp.sum(prob.reshape(CHUNK // 8, 8, LANES), axis=0)
 
-        total = lax.fori_loop(0, last + 1, prob_step, jnp.zeros((8, LANES), F32))
+        total = lax.fori_loop(0, steps, prob_step, jnp.zeros((8, LANES), F32))
         inverse = 1.0 / jnp.sum(total, axis=0, keepdims=True)
         valid = jnp.concatenate(valids, axis=1)
         out_t = (acc_s[...] * (inverse * valid)).astype(BF16)
@@ -181,7 +201,7 @@
             acc_s[...] += dot(kt_s[c], score_grad)
             return carry
 
-        lax.fori_loop(0, last + 1, back_step, 0)
+        lax.fori_loop(0, steps, back_step, 0)
         dq_t = (acc_s[...] * SCALE).astype(BF16)
         for j in range(2):
             for h in range(GROUP):
@@ -211,12 +231,12 @@
         query_grad[:, at] = od[:, HALF:]
 
 
-def sum_kernel(dkv, key_grad, value_grad, share):
+def sum_kernel(info, dkv, key_grad, value_grad, share):
+    core = info[2]
     for h in range(KV_HEADS):
-        first = (h // 2) * 8 + h % 2
-        both = dkv[first].astype(F32)
-        for z in range(1, 4):
-            both = both + dkv[first + 2 * z].astype(F32)
+        both = dkv[block_of(h, 0, core)].astype(F32)
+        for quad in range(1, 4):
+            both = both + dkv[block_of(h, quad, core)].astype(F32)
         both = both.astype(BF16)
         key_grad[:, head_at(h)] = both[:ROWS, :HEAD_DIM]
         value_grad[:, head_at(h)] = both[:ROWS, HEAD_DIM:]
@@ -232,7 +252,7 @@
     return pl.pallas_call(
         attn_kernel,
         out_shape=(bf16(ROWS, LANES),) * 4 + (bf16(16, BOTH, 2 * HEAD_DIM),),
-        in_specs=[SMEM, SMEM] + [VMEM] * 5,
+        in_specs=[SMEM, SMEM] + [VMEM] * len(operands),
         out_specs=(VMEM,) * 5,
         scratch_shapes=[
             pltpu.VMEM((KEYS, HEAD_DIM), BF16),
@@ -266,8 +286,21 @@
     return lax.ppermute(x, axis, [(i, (i + step) % size) for i in range(size)])
 
 
+def local_permute(x, place):
+    pairs = []
+    for i in range(32):
+        xh, z, core = i // 16, i // 2 % 8, i % 2
+        xh, z = place(xh, (z - core) % 8)
+        pairs.append((i, (xh * 8 + (z + core) % 8) * 2 + core))
+    return lax.ppermute(x, LOCAL, pairs)
+
+
 def partner(x, d):
-    return lax.ppermute(x, QUAD, [(i, i ^ d) for i in range(4)])
+    return local_permute(x, lambda xh, z: (xh ^ (d // 2), z ^ (d & 1)))
+
+
+def quad_turn(x, step):
+    return local_permute(x, lambda xh, z: (xh, (z + 2 * step) % 8))
 
 
 def rounded(x):
@@ -275,25 +308,31 @@
 
 
 def body(q_resp, k_resp, v_resp, k_prompt, v_prompt, d_out, lengths, counts):
-    mine = (lax.axis_index("xh") * 2 + lax.axis_index("zl")).astype(jnp.int32)
-    zh = lax.axis_index("zh").astype(jnp.int32)
-    info = jnp.stack([mine, zh, lengths[0], counts[0]])
+    core = lax.axis_index("core")
+    z = (lax.axis_index("z") - core) & 7
+    mine = lax.axis_index("xh") * 2 + (z & 1)
+    info = jnp.stack([mine, z // 2, core, lengths[0], counts[0]]).astype(jnp.int32)
     weight = (RESP_LEN / counts[0].astype(F32)).reshape(1)
-    qd = pl.pallas_call(
+    packed = pl.pallas_call(
         pack_kernel,
-        out_shape=(bf16(ROWS, LANES),) * 4 + (bf16(16, BOTH, 2 * HEAD_DIM),),
+        out_shape=(bf16(ROWS, LANES),) * 4 + (bf16(BOTH, 2 * HEAD_DIM),) * 4,
         in_specs=[SMEM] + [VMEM] * 6,
-        out_specs=(VMEM,) * 5,
+        out_specs=(VMEM,) * 8,
     )(info, q_resp[0], d_out[0], k_resp[0], v_resp[0], k_prompt, v_prompt)
-    qd, kv = list(qd[:4]), qd[4]
+    qd, kv = list(packed[:4]), list(packed[4:])
+    for d in (3, 1, 2):
+        kv[d] = partner(kv[d], d)
     for d in (3, 1, 2):
         qd[d] = partner(qd[d], d)
-    kv = lax.all_to_all(kv, CTX, 0, 0, tiled=True)
-    od = attend(info, weight, *qd, kv)
+    own = jnp.stack(kv)
+    left, right = quad_turn(own, 1), quad_turn(own, -1)
+    far0, far1 = quad_turn(left[:2], 1), quad_turn(right[2:], -1)
+    od = attend(info, weight, *qd, *kv, left, right, far0, far1)
     od, dkv = list(od[:4]), od[4]
     for d in (3, 1, 2):
         od[d] = partner(od[d], d)
     dkv = lax.all_to_all(dkv, CTX, 0, 0, tiled=True)
+    dkv, *od = lax.optimization_barrier((dkv, *od))
     attended, query_grad = pl.pallas_call(
         unpack_kernel,
         out_shape=(bf16(ROWS, HEADS * HEAD_DIM),) * 2,
@@ -304,9 +343,9 @@
     key_grad, value_grad, share = pl.pallas_call(
         sum_kernel,
         out_shape=(bf16(ROWS, width), bf16(ROWS, width), bf16(PROWS, 2 * width)),
-        in_specs=[VMEM],
+        in_specs=[SMEM, VMEM],
         out_specs=(VMEM,) * 3,
-    )(dkv)
+    )(info, dkv)
     for axis in ("core", "xl"):
         share = rounded(share.astype(F32) + swap(share, axis).astype(F32))
     across = share.astype(F32) + turn(share, "y", 2).astype(F32)
@@ -323,7 +362,7 @@
 
 
 def solution(mesh):
-    split = Mesh(mesh.devices.reshape(2, 4, 2, 4, 2, 2), CTX + RESP)
+    split = Mesh(mesh.devices.reshape(2, 8, 4, 2, 2), CTX + RESP)
     rows = P(RESP, CTX, None)
     prompt = P(CTX, None)
     return jax.shard_map(

time: 163 us -> 159 us (0.975)
  blocking collectives: 48.1 us -> 0 us
  waiting for transfers between devices: 50.5 us -> 80.7 us
  starting transfers between devices: 29.3 us -> 37.9 us
  Pallas kernels: 27.4 us -> 32.6 us
    all_to_all x1 -> x0, blocking collectives: 48.1 us -> none  [body(): dkv = lax.all_to_all(dkv, CTX, 0, 0, tiled=True)]
    ppermute x6 -> x13, waiting for transfers between devices: 49 us -> 70.6 us  [local_permute(): return lax.ppermute(x, LOCAL, pairs)]
    ppermute x6 -> x13, starting transfers between devices: 8.39 us -> 25 us  [local_permute(): return lax.ppermute(x, LOCAL, pairs)]
    pallas_call x1, Pallas kernels: 20 us -> 25.6 us  [attend(): pl.pallas_call(attn_kernel, out_shape=(bf16(ROWS, LANES),) * 4 + (bf16(16...]
    ppermute x3, waiting for transfers between devices: 0.01 us -> 4.72 us  [turn(): return lax.ppermute(x, axis, [(i, (i + step) % size) for i in range(size)])]
    all_to_all x1, starting transfers between devices: 11.7 us -> 7.14 us  [body(): dkv = lax.all_to_all(dkv, CTX, 0, 0, tiled=True)]
    ppermute x2, waiting for transfers between devices: 1.45 us -> 5.33 us  [swap(): return lax.ppermute(x, axis, [(0, 1), (1, 0)])]
    ppermute x2, starting transfers between devices: 3.52 us -> 1.26 us  [swap(): return lax.ppermute(x, axis, [(0, 1), (1, 0)])]
  transfers between devices with their start and end apart: 12 -> 19, of which waited for: 5 -> 10; matrix products, arithmetic and copies ran while one was open for 0% -> 0% of each run, Pallas kernels for 1% -> 1%
where the time goes in v3:
time: 159 us
  waiting for transfers between devices  80.7 us (51%)
  starting transfers between devices  37.9 us (24%)
  Pallas kernels  32.6 us (21%)
  local copies, waits for them, and re-layouts  3.27 us (2%)
  between operations  2.07 us (1%)
  other arithmetic  1.99 us (1%)
    ppermute x13, waiting for transfers between devices, local_permute(): return lax.ppermute(x, LOCAL, pairs)  70.6 us
    pallas_call x1, Pallas kernels, attend(): pl.pallas_call(attn_kernel, out_shape=(bf16(ROWS, LANES),) * 4 + (bf16(16...  25.6 us
    ppermute x13, starting transfers between devices, local_permute(): return lax.ppermute(x, LOCAL, pairs)  25 us
    all_to_all x1, starting transfers between devices, body(): dkv = lax.all_to_all(dkv, CTX, 0, 0, tiled=True)  7.14 us
    ppermute x2, waiting for transfers between devices, swap(): return lax.ppermute(x, axis, [(0, 1), (1, 0)])  5.33 us
    ppermute x3, waiting for transfers between devices, turn(): return lax.ppermute(x, axis, [(i, (i + step) % size) for i in range(size)])  4.72 us
    ppermute x3, starting transfers between devices, turn(): return lax.ppermute(x, axis, [(i, (i + step) % size) for i in range(size)])  4.44 us
  transfers between devices with their start and end apart: 19, of which 10 were waited for; matrix products, arithmetic and copies ran while one was open for 0% of the time, Pallas kernels for 1%

profile of v3, /device:TPU:1, one launch (start us, length us, event | category | flops | bytes accessed | tf_op | source)
XLA Modules:
  0.0 158.5 jit_solution(3912955273972151339)
XLA Ops:
  1.9 0.6 stack.30.info
  2.6 2.5 %shard_map.127 = (bf16[128,1024]{1,0:T(8,128)(2,1)}, bf16[128,1024]{1,0:T(8,128)(2,1)}, bf16[128,1024]{1,0:T(8,128)(2,1)}, bf16[128,1024]{1,0:T(8,128)(2,1)}, bf...) custom-call(s32[5]{0:T(128)} %stack.30.info, ...), custom_call_target="tpu_custom_call" | custom-call | tf_op jit(solution)/shard_map/pallas_call | solution.py:316
  5.1 6.5 %collective-permute-start.3 = (bf16[192,256]{1,0:T(8,128)(2,1)}, bf16[192,256]{1,0:T(8,128)(2,1)S(1)}, u32[]{:S(2)}, u32[]{:S(2)}) collective-permute-start(bf16[192,256]{1,0:T(8,128)(2,1)} %get-tuple-element.34), channel_id=1, source_target_pairs={{0,16},{1,113},{16,0},{17,33},{32,48},{33,17},{48,32},{49,65},{64,... | collective-permute-start | bytes 294920 | tf_op jit(solution)/shard_map/ppermute | solution.py:295
  11.6 2.7 %collective-permute-start.4 = (bf16[192,256]{1,0:T(8,128)(2,1)}, bf16[192,256]{1,0:T(8,128)(2,1)S(1)}, u32[]{:S(2)}, u32[]{:S(2)}) collective-permute-start(bf16[192,256]{1,0:T(8,128)(2,1)} %get-tuple-element.35), channel_id=1, source_target_pairs={{0,128},{1,129},{16,144},{17,145},{32,160},{33,161},{48,176},{49,1... | collective-permute-start | bytes 294920 | tf_op jit(solution)/shard_map/ppermute | solution.py:295
  14.3 2.4 %collective-permute-done.4.kv2 = bf16[192,256]{1,0:T(8,128)(2,1)S(1)} collective-permute-done((bf16[192,256]{1,0:T(8,128)(2,1)}, bf16[192,256]{1,0:T(8,128)(2,1)S(1)}, u32[]{:S(2)}, u32[]{:S(2)}) %collective-permute-start.4) | collective-permute-done | bytes 98336 | tf_op jit(solution)/shard_map/ppermute | solution.py:295
  16.7 4.9 %collective-permute-done.5.kv3 = bf16[192,256]{1,0:T(8,128)(2,1)S(1)} collective-permute-done((bf16[192,256]{1,0:T(8,128)(2,1)}, bf16[192,256]{1,0:T(8,128)(2,1)S(1)}, u32[]{:S(2)}, u32[]{:S(2)}) %collective-permute-start.5) | collective-permute-done | bytes 98336 | tf_op jit(solution)/shard_map/ppermute | solution.py:295
  21.6 0.9 pad_maximum_fusion
  22.6 2.4 %collective-permute-start.6 = (bf16[4,192,256]{2,1,0:T(8,128)(2,1)S(1)}, bf16[4,192,256]{2,1,0:T(8,128)(2,1)S(1)}, u32[]{:S(2)}, u32[]{:S(2)}) collective-permute-start(bf16[4,192,256]{2,1,0:T(8,128)(2,1)S(1)} %pad_maximum_fusion), channel_id=1, source_target_pairs={{0,32},{1,33},{16,48},{17,49},{32,64},{33,65},{48,80},{49,81},{64,... | collective-permute-start | bytes 1179656 | tf_op jit(solution)/shard_map/ppermute | solution.py:295
  25.0 1.3 collective-permute-start
  26.6 3.7 %collective-permute-start.2 = (bf16[128,1024]{1,0:T(8,128)(2,1)}, bf16[128,1024]{1,0:T(8,128)(2,1)S(1)}, u32[]{:S(2)}, u32[]{:S(2)}) collective-permute-start(bf16[128,1024]{1,0:T(8,128)(2,1)} %get-tuple-element.32), channel_id=1, source_target_pairs={{0,144},{1,241},{16,128},{17,161},{32,176},{33,145},{48,160},{49,1... | collective-permute-start | bytes 786440 | tf_op jit(solution)/shard_map/ppermute | solution.py:295
  30.3 10.3 %collective-permute-done.7.kv_right = bf16[4,192,256]{2,1,0:T(8,128)(2,1)S(1)} collective-permute-done((bf16[4,192,256]{2,1,0:T(8,128)(2,1)S(1)}, bf16[4,192,256]{2,1,0:T(8,128)(2,1)S(1)}, u32[]{:S(2)}, u32[]{:S(2)}) %collective-permute-start.7) | collective-permute-done | bytes 393248 | tf_op jit(solution)/shard_map/ppermute | solution.py:295
  40.9 2.3 %collective-permute-start.8 = (bf16[2,192,256]{2,1,0:T(8,128)(2,1)S(1)}, bf16[2,192,256]{2,1,0:T(8,128)(2,1)S(1)}, u32[]{:S(2)}, u32[]{:S(2)}) collective-permute-start(bf16[2,192,256]{2,1,0:T(8,128)(2,1)S(1)} %slice.16), channel_id=1, source_target_pairs={{0,32},{1,33},{16,48},{17,49},{32,64},{33,65},{48,80},{49,81},{64,... | collective-permute-start | bytes 589832 | tf_op jit(solution)/shard_map/ppermute | solution.py:295
  43.3 5.3 %collective-permute-done.qd1 = bf16[128,1024]{1,0:T(8,128)(2,1)S(1)} collective-permute-done((bf16[128,1024]{1,0:T(8,128)(2,1)}, bf16[128,1024]{1,0:T(8,128)(2,1)S(1)}, u32[]{:S(2)}, u32[]{:S(2)}) %collective-permute-start) | collective-permute-done | bytes 262176 | tf_op jit(solution)/shard_map/ppermute | solution.py:295
  48.6 6.8 %collective-permute-done.2.qd3 = bf16[128,1024]{1,0:T(8,128)(2,1)S(1)} collective-permute-done((bf16[128,1024]{1,0:T(8,128)(2,1)}, bf16[128,1024]{1,0:T(8,128)(2,1)S(1)}, u32[]{:S(2)}, u32[]{:S(2)}) %collective-permute-start.2) | collective-permute-done | bytes 262176 | tf_op jit(solution)/shard_map/ppermute | solution.py:295
  55.4 25.6 %shard_map.128 = (bf16[128,1024]{1,0:T(8,128)(2,1)S(1)}, bf16[128,1024]{1,0:T(8,128)(2,1)S(1)}, bf16[128,1024]{1,0:T(8,128)(2,1)S(1)}, bf16[128,1024]{1,0:T(8,128)(2,1)S(1)}, bf16[16,192,256]{2,1,0:T(8,128)(2,1)}) custom-call(s32[5]{0:T(128)S(1)} %copy-done.2, f32[1]{0:T(128)S(6)} %div.15.weight, bf16[128,1024]{1,0:T(8,128)(2,1)S(1)} %copy-done.3, ...), custom_call_target="tpu_custom_call" | custom-call | flops 8000000000 | bytes 6000000 | tf_op jit(solution)/shard_map/pallas_call | solution.py:252
  81.0 0.7 copy-done
  81.7 7.1 %all-to-all-start = ((bf16[16,192,256]{2,1,0:T(8,128)(2,1)}), bf16[16,192,256]{2,1,0:T(8,128)(2,1)S(1)}, u32[]{:S(2)}, u32[]{:S(2)}) async-start(bf16[16,192,256]{2,1,0:T(8,128)(2,1)} %get-tuple-element.37), calls=%async_computation | async-start | bytes 3145728 | tf_op jit(solution)/shard_map/all_to_all | solution.py:334
  88.9 2.6 %collective-permute-start.10 = (bf16[128,1024]{1,0:T(8,128)(2,1)S(1)}, bf16[128,1024]{1,0:T(8,128)(2,1)S(1)}, u32[]{:S(2)}, u32[]{:S(2)}) collective-permute-start(bf16[128,1024]{1,0:T(8,128)(2,1)S(1)} %get-tuple-element.39), channel_id=1, source_target_pairs={{0,16},{1,113},{16,0},{17,33},{32,48},{33,17},{48,32},{49,65},{64,... | collective-permute-start | bytes 786440 | tf_op jit(solution)/shard_map/ppermute | solution.py:295
  91.5 2.7 %collective-permute-start.11 = (bf16[128,1024]{1,0:T(8,128)(2,1)S(1)}, bf16[128,1024]{1,0:T(8,128)(2,1)S(1)}, u32[]{:S(2)}, u32[]{:S(2)}) collective-permute-start(bf16[128,1024]{1,0:T(8,128)(2,1)S(1)} %get-tuple-element.40), channel_id=1, source_target_pairs={{0,128},{1,129},{16,144},{17,145},{32,160},{33,161},{48,176},{49,1... | collective-permute-start | bytes 786440 | tf_op jit(solution)/shard_map/ppermute | solution.py:295
  94.3 34.2 %collective-permute-done.10.od1 = bf16[128,1024]{1,0:T(8,128)(2,1)S(1)} collective-permute-done((bf16[128,1024]{1,0:T(8,128)(2,1)S(1)}, bf16[128,1024]{1,0:T(8,128)(2,1)S(1)}, u32[]{:S(2)}, u32[]{:S(2)}) %collective-permute-start.10) | collective-permute-done | bytes 262176 | tf_op jit(solution)/shard_map/ppermute | solution.py:295
  128.5 6.8 %collective-permute-done.12.od3 = bf16[128,1024]{1,0:T(8,128)(2,1)S(1)} collective-permute-done((bf16[128,1024]{1,0:T(8,128)(2,1)S(1)}, bf16[128,1024]{1,0:T(8,128)(2,1)S(1)}, u32[]{:S(2)}, u32[]{:S(2)}) %collective-permute-start.12) | collective-permute-done | bytes 262176 | tf_op jit(solution)/shard_map/ppermute | solution.py:295
  135.3 1.2 copy-done.4
  136.5 2.3 %shard_map.130 = (bf16[128,512]{1,0:T(8,128)(2,1)}, bf16[128,512]{1,0:T(8,128)(2,1)}, bf16[64,1024]{1,0:T(8,128)(2,1)}) custom-call(s32[5]{0:T(128)} %stack.30.info, bf16[16,192,256]{2,1,0:T(8,128)(2,1)} %copy-done.4), custom_call_target="tpu_custom_call" | custom-call | tf_op jit(solution)/shard_map/pallas_call | solution.py:343
  138.8 1.6 collective-permute-done.13
  140.4 0.9 add_convert_fusion.2
  141.3 1.3 collective-permute-start.14
  142.6 3.8 %collective-permute-done.14 = bf16[64,1024]{1,0:T(8,128)(2,1)S(1)} collective-permute-done((bf16[64,1024]{1,0:T(8,128)(2,1)S(1)}, bf16[64,1024]{1,0:T(8,128)(2,1)S(1)}, u32[]{:S(2)}, u32[]{:S(2)}) %collective-permute-start.14) | collective-permute-done | bytes 131104 | tf_op jit(solution)/shard_map/ppermute | solution.py:281
  146.4 2.8 %collective-permute-start.17 = (bf16[64,1024]{1,0:T(8,128)(2,1)S(1)}, bf16[64,1024]{1,0:T(8,128)(2,1)S(1)}, u32[]{:S(2)}, u32[]{:S(2)}) collective-permute-start(bf16[64,1024]{1,0:T(8,128)(2,1)S(1)} %add_convert_fusion.1), channel_id=1, source_target_pairs={{0,12},{4,0},{8,4},{12,8},{1,13},{5,1},{9,5},{13,9},{2,14},{6,2},{... | collective-permute-start | bytes 393224 | tf_op jit(solution)/shard_map/ppermute | solution.py:286
  149.2 1.6 %collective-permute-start.15 = (bf16[64,1024]{1,0:T(8,128)(2,1)S(1)}, bf16[64,1024]{1,0:T(8,128)(2,1)S(1)}, u32[]{:S(2)}, u32[]{:S(2)}) collective-permute-start(bf16[64,1024]{1,0:T(8,128)(2,1)S(1)} %add_convert_fusion.1), channel_id=1, source_target_pairs={{0,8},{4,12},{8,0},{12,4},{1,9},{5,13},{9,1},{13,5},{2,10},{6,14},... | collective-permute-start | bytes 393224 | tf_op jit(solution)/shard_map/ppermute | solution.py:286
  150.8 2.2 %shard_map.129 = (bf16[128,2048]{1,0:T(8,128)(2,1)}, bf16[128,2048]{1,0:T(8,128)(2,1)}) custom-call(s32[5]{0:T(128)} %stack.30.info, bf16[128,1024]{1,0:T(8,128)(2,1)} %copy-done, bf16[128,1024]{1,0:T(8,128)(2,1)} %copy-done.5, bf16[128,1024]{1,0:T(8,128)(2,1)} %copy-done.6, bf16[128,1024]{1,0:T(8,128)(2,1)} %copy-done.7), custom_call_target="tpu_custom_call" | custom-call | tf_op jit(solution)/shard_map/pallas_call | solution.py:336
  153.1 4.7 %collective-permute-done.16 = bf16[64,1024]{1,0:T(8,128)(2,1)S(1)} collective-permute-done((bf16[64,1024]{1,0:T(8,128)(2,1)S(1)}, bf16[64,1024]{1,0:T(8,128)(2,1)S(1)}, u32[]{:S(2)}, u32[]{:S(2)}) %collective-permute-start.16) | collective-permute-done | bytes 131104 | tf_op jit(solution)/shard_map/ppermute | solution.py:286
  157.9 0.7 fusion
  (34 shorter events, 1.0 us)
Async XLA Ops:
  2.5 52.8 %copy-start.2 = (s32[5]{0:T(128)S(1)}, s32[5]{0:T(128)}, u32[]{:S(2)}) copy-start(s32[5]{0:T(128)} %stack.30.info) | copy-start | bytes 64
  5.1 50.3 %copy-start.1 = (bf16[192,256]{1,0:T(8,128)(2,1)S(1)}, bf16[192,256]{1,0:T(8,128)(2,1)}, u32[]{:S(2)}) copy-start(bf16[192,256]{1,0:T(8,128)(2,1)} %get-tuple-element.33.kv0) | copy-start | bytes 294916
  5.1 50.3 %copy-start.3 = (bf16[128,1024]{1,0:T(8,128)(2,1)S(1)}, bf16[128,1024]{1,0:T(8,128)(2,1)}, u32[]{:S(2)}) copy-start(bf16[128,1024]{1,0:T(8,128)(2,1)} %get-tuple-element.29.qd0) | copy-start | bytes 786436
  5.1 9.3 %collective-permute-start.3 = (bf16[192,256]{1,0:T(8,128)(2,1)}, bf16[192,256]{1,0:T(8,128)(2,1)S(1)}, u32[]{:S(2)}, u32[]{:S(2)}) collective-permute-start(bf16[192,256]{1,0:T(8,128)(2,1)} %get-tuple-element.34), channel_id=1, source_target_pairs={{0,16},{1,113},{16,0},{17,33},{32,48},{33,17},{48,32},{49,65},{64,... | collective-permute-start | bytes 294920 | tf_op jit(solution)/shard_map/ppermute | solution.py:295
  11.6 5.2 %collective-permute-start.4 = (bf16[192,256]{1,0:T(8,128)(2,1)}, bf16[192,256]{1,0:T(8,128)(2,1)S(1)}, u32[]{:S(2)}, u32[]{:S(2)}) collective-permute-start(bf16[192,256]{1,0:T(8,128)(2,1)} %get-tuple-element.35), channel_id=1, source_target_pairs={{0,128},{1,129},{16,144},{17,145},{32,160},{33,161},{48,176},{49,1... | collective-permute-start | bytes 294920 | tf_op jit(solution)/shard_map/ppermute | solution.py:295
  14.3 7.3 %collective-permute-start.5 = (bf16[192,256]{1,0:T(8,128)(2,1)}, bf16[192,256]{1,0:T(8,128)(2,1)S(1)}, u32[]{:S(2)}, u32[]{:S(2)}) collective-permute-start(bf16[192,256]{1,0:T(8,128)(2,1)} %get-tuple-element.36), channel_id=1, source_target_pairs={{0,144},{1,241},{16,128},{17,161},{32,176},{33,145},{48,160},{49,1... | collective-permute-start | bytes 294920 | tf_op jit(solution)/shard_map/ppermute | solution.py:295
  22.5 18.1 %collective-permute-start.7 = (bf16[4,192,256]{2,1,0:T(8,128)(2,1)S(1)}, bf16[4,192,256]{2,1,0:T(8,128)(2,1)S(1)}, u32[]{:S(2)}, u32[]{:S(2)}) collective-permute-start(bf16[4,192,256]{2,1,0:T(8,128)(2,1)S(1)} %pad_maximum_fusion), channel_id=1, source_target_pairs={{0,96},{1,97},{16,112},{17,113},{32,0},{33,1},{48,16},{49,17},{64,... | collective-permute-start | bytes 1179656 | tf_op jit(solution)/shard_map/ppermute | solution.py:295
  22.6 18.3 %collective-permute-start.6 = (bf16[4,192,256]{2,1,0:T(8,128)(2,1)S(1)}, bf16[4,192,256]{2,1,0:T(8,128)(2,1)S(1)}, u32[]{:S(2)}, u32[]{:S(2)}) collective-permute-start(bf16[4,192,256]{2,1,0:T(8,128)(2,1)S(1)} %pad_maximum_fusion), channel_id=1, source_target_pairs={{0,32},{1,33},{16,48},{17,49},{32,64},{33,65},{48,80},{49,81},{64,... | collective-permute-start | bytes 1179656 | tf_op jit(solution)/shard_map/ppermute | solution.py:295
  25.0 23.6 %collective-permute-start = (bf16[128,1024]{1,0:T(8,128)(2,1)}, bf16[128,1024]{1,0:T(8,128)(2,1)S(1)}, u32[]{:S(2)}, u32[]{:S(2)}) collective-permute-start(bf16[128,1024]{1,0:T(8,128)(2,1)} %get-tuple-element.30), channel_id=1, source_target_pairs={{0,16},{1,113},{16,0},{17,33},{32,48},{33,17},{48,32},{49,65},{64,... | collective-permute-start | bytes 786440 | tf_op jit(solution)/shard_map/ppermute | solution.py:295
  26.3 22.3 %collective-permute-start.1 = (bf16[128,1024]{1,0:T(8,128)(2,1)}, bf16[128,1024]{1,0:T(8,128)(2,1)S(1)}, u32[]{:S(2)}, u32[]{:S(2)}) collective-permute-start(bf16[128,1024]{1,0:T(8,128)(2,1)} %get-tuple-element.31), channel_id=1, source_target_pairs={{0,128},{1,129},{16,144},{17,145},{32,160},{33,161},{48,176},{49,1... | collective-permute-start | bytes 786440 | tf_op jit(solution)/shard_map/ppermute | solution.py:295
  26.6 28.8 %collective-permute-start.2 = (bf16[128,1024]{1,0:T(8,128)(2,1)}, bf16[128,1024]{1,0:T(8,128)(2,1)S(1)}, u32[]{:S(2)}, u32[]{:S(2)}) collective-permute-start(bf16[128,1024]{1,0:T(8,128)(2,1)} %get-tuple-element.32), channel_id=1, source_target_pairs={{0,144},{1,241},{16,128},{17,161},{32,176},{33,145},{48,160},{49,1... | collective-permute-start | bytes 786440 | tf_op jit(solution)/shard_map/ppermute | solution.py:295
  40.7 14.7 %collective-permute-start.9 = (bf16[2,192,256]{2,1,0:T(8,128)(2,1)S(1)}, bf16[2,192,256]{2,1,0:T(8,128)(2,1)S(1)}, u32[]{:S(2)}, u32[]{:S(2)}) collective-permute-start(bf16[2,192,256]{2,1,0:T(8,128)(2,1)S(1)} %slice.17), channel_id=1, source_target_pairs={{0,96},{1,97},{16,112},{17,113},{32,0},{33,1},{48,16},{49,17},{64,... | collective-permute-start | bytes 589832 | tf_op jit(solution)/shard_map/ppermute | solution.py:295
  40.9 14.5 %collective-permute-start.8 = (bf16[2,192,256]{2,1,0:T(8,128)(2,1)S(1)}, bf16[2,192,256]{2,1,0:T(8,128)(2,1)S(1)}, u32[]{:S(2)}, u32[]{:S(2)}) collective-permute-start(bf16[2,192,256]{2,1,0:T(8,128)(2,1)S(1)} %slice.16), channel_id=1, source_target_pairs={{0,32},{1,33},{16,48},{17,49},{32,64},{33,65},{48,80},{49,81},{64,... | collective-permute-start | bytes 589832 | tf_op jit(solution)/shard_map/ppermute | solution.py:295
  81.0 0.7 copy-start
  81.7 53.6 %all-to-all-start = ((bf16[16,192,256]{2,1,0:T(8,128)(2,1)}), bf16[16,192,256]{2,1,0:T(8,128)(2,1)S(1)}, u32[]{:S(2)}, u32[]{:S(2)}) async-start(bf16[16,192,256]{2,1,0:T(8,128)(2,1)} %get-tuple-element.37), calls=%async_computation | async-start | bytes 3145728 | tf_op jit(solution)/shard_map/all_to_all | solution.py:334
  88.9 39.6 %collective-permute-start.10 = (bf16[128,1024]{1,0:T(8,128)(2,1)S(1)}, bf16[128,1024]{1,0:T(8,128)(2,1)S(1)}, u32[]{:S(2)}, u32[]{:S(2)}) collective-permute-start(bf16[128,1024]{1,0:T(8,128)(2,1)S(1)} %get-tuple-element.39), channel_id=1, source_target_pairs={{0,16},{1,113},{16,0},{17,33},{32,48},{33,17},{48,32},{49,65},{64,... | collective-permute-start | bytes 786440 | tf_op jit(solution)/shard_map/ppermute | solution.py:295
  91.5 37.1 %collective-permute-start.11 = (bf16[128,1024]{1,0:T(8,128)(2,1)S(1)}, bf16[128,1024]{1,0:T(8,128)(2,1)S(1)}, u32[]{:S(2)}, u32[]{:S(2)}) collective-permute-start(bf16[128,1024]{1,0:T(8,128)(2,1)S(1)} %get-tuple-element.40), channel_id=1, source_target_pairs={{0,128},{1,129},{16,144},{17,145},{32,160},{33,161},{48,176},{49,1... | collective-permute-start | bytes 786440 | tf_op jit(solution)/shard_map/ppermute | solution.py:295
  94.2 41.1 %collective-permute-start.12 = (bf16[128,1024]{1,0:T(8,128)(2,1)S(1)}, bf16[128,1024]{1,0:T(8,128)(2,1)S(1)}, u32[]{:S(2)}, u32[]{:S(2)}) collective-permute-start(bf16[128,1024]{1,0:T(8,128)(2,1)S(1)} %get-tuple-element.41), channel_id=1, source_target_pairs={{0,144},{1,241},{16,128},{17,161},{32,176},{33,145},{48,160},{49,1... | collective-permute-start | bytes 786440 | tf_op jit(solution)/shard_map/ppermute | solution.py:295
  128.5 22.3 %copy-start.5 = (bf16[128,1024]{1,0:T(8,128)(2,1)}, bf16[128,1024]{1,0:T(8,128)(2,1)S(1)}, u32[]{:S(2)}) copy-start(bf16[128,1024]{1,0:T(8,128)(2,1)S(1)} %collective-permute-done.10.od1) | copy-start | bytes 786436
  128.5 22.3 %copy-start.6 = (bf16[128,1024]{1,0:T(8,128)(2,1)}, bf16[128,1024]{1,0:T(8,128)(2,1)S(1)}, u32[]{:S(2)}) copy-start(bf16[128,1024]{1,0:T(8,128)(2,1)S(1)} %collective-permute-done.11.od2) | copy-start | bytes 786436
  135.3 15.6 %copy-start.7 = (bf16[128,1024]{1,0:T(8,128)(2,1)}, bf16[128,1024]{1,0:T(8,128)(2,1)S(1)}, u32[]{:S(2)}) copy-start(bf16[128,1024]{1,0:T(8,128)(2,1)S(1)} %collective-permute-done.12.od3) | copy-start | bytes 786436
  135.3 1.2 copy-start.4
  138.8 1.6 collective-permute-start.13
  141.3 5.0 %collective-permute-start.14 = (bf16[64,1024]{1,0:T(8,128)(2,1)S(1)}, bf16[64,1024]{1,0:T(8,128)(2,1)S(1)}, u32[]{:S(2)}, u32[]{:S(2)}) collective-permute-start(bf16[64,1024]{1,0:T(8,128)(2,1)S(1)} %add_convert_fusion.2), channel_id=1, source_target_pairs={{0,2},{2,0},{1,3},{3,1},{4,6},{6,4},{5,7},{7,5},{8,10},{10,8},{9,1... | collective-permute-start | bytes 393224 | tf_op jit(solution)/shard_map/ppermute | solution.py:281
  146.4 6.7 %collective-permute-start.17 = (bf16[64,1024]{1,0:T(8,128)(2,1)S(1)}, bf16[64,1024]{1,0:T(8,128)(2,1)S(1)}, u32[]{:S(2)}, u32[]{:S(2)}) collective-permute-start(bf16[64,1024]{1,0:T(8,128)(2,1)S(1)} %add_convert_fusion.1), channel_id=1, source_target_pairs={{0,12},{4,0},{8,4},{12,8},{1,13},{5,1},{9,5},{13,9},{2,14},{6,2},{... | collective-permute-start | bytes 393224 | tf_op jit(solution)/shard_map/ppermute | solution.py:286
  149.2 8.6 %collective-permute-start.16 = (bf16[64,1024]{1,0:T(8,128)(2,1)S(1)}, bf16[64,1024]{1,0:T(8,128)(2,1)S(1)}, u32[]{:S(2)}, u32[]{:S(2)}) collective-permute-start(bf16[64,1024]{1,0:T(8,128)(2,1)S(1)} %add_convert_fusion.1), channel_id=1, source_target_pairs={{0,4},{4,8},{8,12},{12,0},{1,5},{5,9},{9,13},{13,1},{2,6},{6,10},{... | collective-permute-start | bytes 393224 | tf_op jit(solution)/shard_map/ppermute | solution.py:286
  149.2 8.6 %collective-permute-start.15 = (bf16[64,1024]{1,0:T(8,128)(2,1)S(1)}, bf16[64,1024]{1,0:T(8,128)(2,1)S(1)}, u32[]{:S(2)}, u32[]{:S(2)}) collective-permute-start(bf16[64,1024]{1,0:T(8,128)(2,1)S(1)} %add_convert_fusion.1), channel_id=1, source_target_pairs={{0,8},{4,12},{8,0},{12,4},{1,9},{5,13},{9,1},{13,5},{2,10},{6,14},... | collective-permute-start | bytes 393224 | tf_op jit(solution)/shard_map/ppermute | solution.py:286
